TPU v7x, 32 devices: a whole 2x2x4 slice. The times are simulated.
32 devices in a mesh: basin: 8 (over z, x), event: 4 (over y, core).
Axes of the slice: x: 2, y: 2, z: 4, core: 2. Of those that a mesh axis runs over, the one named last changes fastest.
Arguments:
- reach_attrs: bfloat16 [12288, 32], P('basin'), may hold values from -6 to 6
- w_first: bfloat16 [32, 768], replicated, may hold values from -1 to 1
- b_first: float32 [768], replicated, may hold values from -3 to 3
- w_second: bfloat16 [768, 768], replicated, may hold values from -0.21875 to 0.21875
- b_second: float32 [768], replicated, may hold values from -3 to 3
- w_out: bfloat16 [768], replicated, may hold values from -0.21875 to 0.21875
- section_factor: float32 [10], replicated, may hold values from 0.5 to 2
- bed_slope: float32 [12288], P('basin'), may hold values from 0.0001 to 0.004
- seg_count: int32 [12288], P('basin'), may hold values from 1 to 8
- section_class: int32 [12288], P('basin'), may hold values from 0 to 9
- down_local: int32 [12288], P('basin'), may hold values from 0 to 1536, as said below
- send_list: int32 [8, 8, 24], P('basin'), may hold values from 0 to 1536, as said below
- recv_list: int32 [8, 8, 24], P('basin'), may hold values from 0 to 1536, as said below
- area_start: float32 [128, 12288], P('event', 'basin'), may hold values from 0.2 to 2
- lateral: float32 [3, 128, 12288], P(None, 'event', 'basin'), may hold values from 0.05 to 1
- cotangent: float32 [128, 12288], P('event', 'basin'), may hold values from -6 to 6
Outputs:
- outflow: float32 [128, 12288], P('event', 'basin')
- grad_lateral: float32 [3, 128, 12288], P(None, 'event', 'basin')
- grad_w_first: float32 [32, 768], replicated
- grad_b_first: float32 [768], replicated
- grad_w_second: float32 [768, 768], replicated
- grad_b_second: float32 [768], replicated
- grad_w_out: float32 [768], replicated
Inputs may be any that keep to these rules, and one draw needn't show every extreme that they name: `down_local`: the downstream reach of a reach in its own sub-basin, as a local index 1 to 8 above the reach's own; 1536 where the reach drains into another sub-basin (it is then listed in send_list) or leaves the network. send_list[s, d, c] is a local reach of sub-basin s whose end flow enters sub-basin d, or 1536 for an empty slot; live slots come first in each list and no reach is listed twice. Only the lists from s to (s + 1), (s + 2), (s + 4) and (s + 7) mod 8 can hold live slots; those to (s + 1), (s + 4) and (s + 7) are always full, the one to (s + 2) is empty or holds 12 or more. One sub-basin receives 24 from each of the four sub-basins that can drain into it. recv_list[d, s, c] is the local reach of sub-basin d that receives slot c of send_list[s, d], and is 1536 exactly where that slot is empty; no reach is a target twice.
All inputs are finite; a program needn't handle non-finite values.
Results may differ from a plain program's by a relative error of at most 0.02.
Values sent between devices are 32-bit elements; how exact they have to be, the bound alone decides.
A program may use at most 64 MiB of HBM per device.

v0:
```python
import functools
import math

import jax
import jax.numpy as jnp
from jax import lax
from jax.experimental import pallas as pl
from jax.experimental.pallas import tpu as pltpu
from jax.sharding import PartitionSpec as P

STEPS = 3
LINKS = 4
GROUP = 32
MESH = pl.DeviceIdType.MESH
NT = (((1,), (1,)), ((), ()))


def split_two(x):
    high = x.astype(jnp.bfloat16)
    low = (x - high.astype(jnp.float32)).astype(jnp.bfloat16)
    return jnp.concatenate([high, low], axis=0)


def kernel(
    n, n_event, owners, chunk, scale,
    w_firstT, w_second, w_secondT, cols, attrs, rows, send_list, recv_list,
    area_start, lateral, cotangent,
    outflow, grad_lateral, full,
    t_one, h_one, d_two, h_two, g_two, squash_row, take_send, take_recv,
    out_msg, in_msg, rate_out, rate_in, slab, rs_pair, rs_line,
    x_send, x_recv, r_send, r_recv, px_send, px_recv, pz_send, pz_recv,
    az_send, az_recv, ax_send, ax_recv, ay_send, ay_recv, ac_send, ac_recv,
    bz_send, bz_recv, bx_send, bx_recv, by_send, by_recv, bc_send, bc_recv,
):
    f32, bf16 = jnp.float32, jnp.bfloat16
    me = lax.axis_index("basin")
    ev = lax.axis_index("event")
    events, reaches = area_start.shape
    hid = w_second.shape[0]
    feat = w_firstT.shape[1]
    part = hid // n_event
    offsets = (1, 2, n // 2, n - 1)
    base = pl.multiple_of(ev * part, 64)

    barrier = pltpu.get_barrier_semaphore()

    @pl.loop(1, n)
    def _(i):
        pl.semaphore_signal(barrier, inc=1, device_id={"basin": lax.rem(me + i, n)}, device_id_type=MESH)

    for i in range(1, n_event):
        pl.semaphore_signal(
            barrier, inc=1, device_id={"event": lax.rem(ev + i, n_event)}, device_id_type=MESH
        )

    tile = 256

    @pl.loop(0, reaches // tile)
    def _(i):
        where = pl.ds(pl.multiple_of(i * tile, tile), tile)
        one = jnp.tanh(
            jnp.dot(w_firstT[...], attrs[0:feat, where], preferred_element_type=f32) + cols[:, 0:1]
        )
        t_one[:, where] = one
        hidden = one.astype(bf16)
        h_one[:, where] = hidden
        two = jnp.tanh(
            jnp.dot(w_secondT[...], hidden, preferred_element_type=f32) + cols[:, 1:2]
        )
        h_two[:, where] = two.astype(bf16)
        d_two[:, where] = cols[:, 2:3] * (1.0 - two * two)
        logit = jnp.sum(two.astype(bf16).astype(f32) * cols[:, 2:3], axis=0, keepdims=True)
        squash_row[:, where] = 1.0 / (1.0 + jnp.exp(-logit))

    slot_row = lax.broadcasted_iota(jnp.int32, (LINKS * GROUP, 1), 0)
    slot = slot_row % GROUP
    cap = send_list.shape[2]
    spread = (
        slot == lax.broadcasted_iota(jnp.int32, (LINKS * GROUP, cap), 1)
    ).astype(f32)
    lane_reach = lax.broadcasted_iota(jnp.int32, (LINKS * GROUP, reaches), 1).astype(f32)
    lane_basin = lax.broadcasted_iota(jnp.int32, (LINKS * GROUP, n), 1)

    def one_hot_of(lists, sign):
        table = lax.dot_general(
            spread, lists[0].astype(f32), NT, precision=lax.Precision.HIGHEST,
            preferred_element_type=f32,
        )
        peer = jnp.zeros((LINKS * GROUP, 1), jnp.int32)
        for k, off in enumerate(offsets):
            peer = jnp.where(slot_row // GROUP == k, lax.rem(me + sign * off + n, n), peer)
        column = jnp.sum(jnp.where(lane_basin == peer, table, 0.0), axis=1, keepdims=True)
        column = jnp.where(slot < cap, column, float(reaches))
        return (jnp.abs(lane_reach - column) < 0.5).astype(bf16)

    take_send[...] = one_hot_of(send_list, 1)
    take_recv[...] = one_hot_of(recv_list, -1)

    squash = squash_row[...]
    rough = 0.02 + 0.08 * squash
    rate = rows[0:1, :] / rough
    beta = rows[1:2, :]
    hop = rows[2:3, :]
    masks = [(jnp.abs(hop - float(d)) < 0.5).astype(f32) for d in range(1, 9)]

    pl.semaphore_wait(barrier, n - 1 + n_event - 1)

    lane_group = lax.broadcasted_iota(jnp.int32, (8, 128), 1) // GROUP
    blocks = events // 8

    def message(index, k, sign):
        return pltpu.make_async_remote_copy(
            src_ref=out_msg.at[index, k],
            dst_ref=in_msg.at[index, k],
            send_sem=x_send.at[index, k],
            recv_sem=x_recv.at[index, k],
            device_id={"basin": lax.rem(me + sign * offsets[k] + n, n)},
            device_id_type=MESH,
        )

    def send(index, field, matrix, sign):
        both = lax.dot_general(split_two(field), matrix[...], NT, preferred_element_type=f32)
        picked = both[:events] + both[events:]
        for k in range(LINKS):
            packed = jnp.zeros((8, 128), f32)
            for q in range(blocks):
                piece = picked[8 * q : 8 * q + 8]
                shift = ((q - k) * GROUP) % 128
                if shift:
                    piece = pltpu.roll(piece, shift, 1)
                packed = jnp.where(lane_group == q, piece, packed)
            out_msg[index, k] = packed
            message(index, k, sign).start()

    def receive(index, matrix, sign):
        for k in range(LINKS):
            message(index, k, sign).wait_recv()
        pieces = []
        for q in range(blocks):
            got = jnp.zeros((8, 128), f32)
            for k in range(LINKS):
                piece = in_msg[index, k]
                shift = ((k - q) * GROUP) % 128
                if shift:
                    piece = pltpu.roll(piece, shift, 1)
                got = jnp.where(lane_group == k, piece, got)
            pieces.append(got)
        both = jnp.dot(
            split_two(jnp.concatenate(pieces, axis=0)), matrix[...], preferred_element_type=f32
        )
        return both[:events] + both[events:]

    def power(area):
        return jnp.exp((2.0 / 3.0) * jnp.log(area))

    areas = [area_start[...]]
    powers = [power(areas[0])]
    shrinks = []
    for t in range(STEPS):
        area, p = areas[t], powers[t]
        flow = rate * area * p
        send(t, flow, take_send, 1)
        inflow = lateral[t]
        for d in range(1, 9):
            inflow = inflow + pltpu.roll(flow * masks[d - 1], d, 1)
        shrink = 1.0 / (1.0 + beta * rate * p)
        shrinks.append(shrink)
        inflow = inflow + receive(t, take_recv, 1)
        areas.append((area + beta * inflow) * shrink)
        powers.append(power(areas[t + 1]))
    emitted = areas[STEPS] * powers[STEPS]
    outflow[...] = rate * emitted
    g_area = cotangent[...] * rate * (5.0 / 3.0) * powers[STEPS]
    g_rate = cotangent[...] * emitted
    for t in reversed(range(STEPS)):
        index = 2 * STEPS - 1 - t
        inner = g_area * shrinks[t]
        g_inflow = inner * beta
        grad_lateral[t] = g_inflow
        send(index, g_inflow, take_recv, -1)
        g_flow = jnp.zeros((events, reaches), f32)
        for d in range(1, 9):
            g_flow = g_flow + masks[d - 1] * pltpu.roll(g_inflow, reaches - d, 1)
        drop = g_inflow * areas[t + 1] * powers[t]
        g_rate = g_rate - drop
        g_area = inner - (2.0 / 3.0) * rate * drop / areas[t]
        g_flow = g_flow + receive(index, take_send, -1)
        g_rate = g_rate + g_flow * areas[t] * powers[t]
        g_area = g_area + (5.0 / 3.0) * rate * powers[t] * g_flow
    rate_out[...] = jnp.sum(g_rate, axis=0, keepdims=True)

    def rate_copy(i):
        return pltpu.make_async_remote_copy(
            src_ref=rate_out,
            dst_ref=rate_in.at[i],
            send_sem=r_send.at[i],
            recv_sem=r_recv.at[i],
            device_id={"event": lax.rem(ev + 1 + i, n_event)},
            device_id_type=MESH,
        )

    for i in range(n_event - 1):
        rate_copy(i).start()
    for i in range(n_event - 1):
        rate_copy(i).wait_recv()
    terms = [rate_out[...]] + [rate_in[i] for i in range(n_event - 1)]
    g_sum = jnp.zeros((1, reaches), f32)
    for e in range(n_event):
        term = terms[0]
        for i in range(n_event - 1):
            term = jnp.where(lax.rem(e + 1 + i, n_event) == ev, terms[i + 1], term)
        g_sum = g_sum + term
    g_logit = (
        g_sum * (-rate / rough) * (scale * 0.08) * squash * (1.0 - squash)
    ).astype(bf16)
    g_logit32 = g_logit.astype(f32)

    @pl.loop(0, hid // 64)
    def _(i):
        where = pl.ds(pl.multiple_of(i * 64, 64), 64)
        g_two[where, :] = (d_two[where, :] * g_logit32).astype(bf16)

    mine = pl.ds(base, part)
    slab[:, 0:hid] = lax.dot_general(h_one[mine, :], g_two[...], NT, preferred_element_type=f32)
    one = t_one[mine, :]
    g_pre = (
        jnp.dot(w_second[mine, :], g_two[...], preferred_element_type=f32) * (1.0 - one * one)
    ).astype(bf16)
    lane_kind = lax.broadcasted_iota(jnp.int32, (128, reaches), 0)
    units = jnp.where(lane_kind == feat + 1, 1.0, 0.0).astype(bf16)
    logits = jnp.where(lane_kind == feat + 2, g_logit32, 0.0).astype(bf16)
    slab[:, hid:] = (
        lax.dot_general(g_pre, attrs[...], NT, preferred_element_type=f32)
        + lax.dot_general(g_two[mine, :], units, NT, preferred_element_type=f32)
        + lax.dot_general(h_two[mine, :], logits, NT, preferred_element_type=f32)
    )

    def when_owner(index, work):
        if owners == n:
            work()
        else:
            pl.when(index < owners)(work)

    def span(index):
        return pl.ds(pl.multiple_of(index * chunk, 8), chunk)

    line = n // 2
    low = lax.rem(me, 2)
    spot = me // 2
    pair = me + 1 - 2 * low
    half = lax.rem(ev + n_event // 2, n_event)
    twin = ev + 1 - 2 * lax.rem(ev, 2)
    twin_half = lax.rem(twin + n_event // 2, n_event)

    def device(z, parity):
        return 2 * z + parity

    def pair_sum(z, parity):
        return pltpu.make_async_remote_copy(
            src_ref=slab.at[span(device(z, parity))], dst_ref=rs_pair.at[z],
            send_sem=px_send.at[z], recv_sem=px_recv.at[z],
            device_id={"basin": pair}, device_id_type=MESH,
        )

    def line_sum(z, sender):
        return pltpu.make_async_remote_copy(
            src_ref=rs_pair.at[z], dst_ref=rs_line.at[sender],
            send_sem=pz_send.at[z], recv_sem=pz_recv.at[sender],
            device_id={"basin": device(z, low)}, device_id_type=MESH,
        )

    for j in range(line):
        z = lax.rem(spot + 1 + j, line)
        when_owner(device(z, 1 - low), lambda z=z: pair_sum(z, 1 - low).start())

    @pl.loop(0, line)
    def _(j):
        z = lax.rem(spot + 1 + j, line)

        def go():
            pair_sum(z, 1 - low).wait_recv()
            rs_pair[z] = rs_pair[z] + slab[span(device(z, low)), :]

            @pl.when(j < line - 1)
            def _():
                line_sum(z, spot).start()

        when_owner(device(z, low), go)

    early = 0
    late = chunk - early

    def rows_a(event, z, parity):
        return full.at[pl.ds(pl.multiple_of(event * part + device(z, parity) * chunk, 8), late)]

    def rows_b(event, z, parity):
        start = event * part + device(z, parity) * chunk + late
        return full.at[pl.ds(pl.multiple_of(start, 8), early)]

    def move(where, send_sem, recv_sem, target):
        return pltpu.make_async_remote_copy(
            src_ref=where, dst_ref=where, send_sem=send_sem, recv_sem=recv_sem,
            device_id=target, device_id_type=MESH,
        )

    def a_line(source, peer):
        return move(rows_a(ev, source, low), az_send.at[peer], az_recv.at[source],
                    {"basin": device(peer, low)})

    def a_pair(z, parity):
        return move(rows_a(ev, z, parity), ax_send.at[z], ax_recv.at[z], {"basin": pair})

    def a_half(event, z, parity):
        at = device(z, parity)
        return move(rows_a(event, z, parity), ay_send.at[at], ay_recv.at[at], {"event": half})

    def a_twin(side, event, z, parity):
        at = device(z, parity)
        return move(rows_a(event, z, parity), ac_send.at[side, at], ac_recv.at[side, at],
                    {"event": twin})

    def b_line(side, source, peer):
        return move(rows_b((ev, half)[side], source, low), bz_send.at[side, peer],
                    bz_recv.at[side, source], {"basin": device(peer, low)})

    def b_pair(side, z, parity):
        return move(rows_b((ev, half)[side], z, parity), bx_send.at[side, z],
                    bx_recv.at[side, z], {"basin": pair})

    def b_half(event):
        return move(rows_b(event, spot, low), by_send, by_recv, {"event": half})

    def b_twin(side, event, z, parity):
        at = device(z, parity)
        return move(rows_b(event, z, parity), bc_send.at[side, at], bc_recv.at[side, at],
                    {"event": twin})

    def a_on(z, parity):
        a_half(ev, z, parity).start()
        a_twin(0, ev, z, parity).start()

    def b_spread(side):
        for j in range(1, line):
            b_line(side, spot, lax.rem(spot + j, line)).start()
        b_pair(side, spot, low).start()
        b_twin(side, (ev, half)[side], spot, low).start()

    def own():
        def add(i, total):
            sender = lax.rem(spot + line - i, line)
            line_sum(spot, sender).wait_recv()
            return total + rs_line[sender]

        full[pl.ds(pl.multiple_of(ev * part + me * chunk, 8), chunk), :] = lax.fori_loop(
            1, line, add, rs_pair[spot]
        )

        a_half(ev, spot, low).start()
        for j in range(1, line):
            a_line(spot, lax.rem(spot + j, line)).start()
        a_pair(spot, low).start()
        a_twin(0, ev, spot, low).start()
        if early:
            b_half(ev).start()
            b_spread(0)

    when_owner(me, own)
    when_owner(pair, lambda: (a_pair(spot, 1 - low).wait_recv(), a_on(spot, 1 - low))[0])
    if early:
        b_half(half).wait_recv()
        b_spread(1)

    @pl.loop(1, line)
    def _(j):
        z = lax.rem(spot + line - j, line)

        def go():
            a_line(z, spot).wait_recv()
            a_half(ev, z, low).start()
            a_pair(z, low).start()
            a_twin(0, ev, z, low).start()

        when_owner(device(z, low), go)

        def go_pair():
            a_pair(z, 1 - low).wait_recv()
            a_on(z, 1 - low)

        when_owner(device(z, 1 - low), go_pair)

    if early:
        for side in range(2):
            event = (ev, half)[side]
            b_pair(side, spot, 1 - low).wait_recv()
            b_twin(side, event, spot, 1 - low).start()

        @pl.loop(1, line)
        def _(j):
            z = lax.rem(spot + line - j, line)
            for side in range(2):
                event = (ev, half)[side]
                b_line(side, z, spot).wait_recv()
                b_pair(side, z, low).start()
                b_twin(side, event, z, low).start()
            for side in range(2):
                event = (ev, half)[side]
                b_pair(side, z, 1 - low).wait_recv()
                b_twin(side, event, z, 1 - low).start()

    @pl.loop(0, line)
    def _(j):
        z = lax.rem(spot + line - j, line)
        for parity in (low, 1 - low):

            def go():
                a_half(half, z, parity).wait_recv()
                a_twin(1, half, z, parity).start()

            when_owner(device(z, parity), go)

    for index in range(2 * STEPS):
        for k in range(LINKS):
            message(index, k, 1).wait_send()
    for i in range(n_event - 1):
        rate_copy(i).wait_send()

    @pl.loop(0, line)
    def _(z):
        when_owner(device(z, 1 - low), lambda: pair_sum(z, 1 - low).wait_send())
        when_owner(device(z, low), lambda: a_pair(z, low).wait_send())

        @pl.when(z != spot)
        def _():
            when_owner(device(z, low), lambda: line_sum(z, spot).wait_send())
            when_owner(me, lambda: a_line(spot, z).wait_send())

        if early:
            for side in range(2):
                b_pair(side, z, low).wait_send()

                @pl.when(z != spot)
                def _():
                    b_line(side, spot, z).wait_send()

        for parity in range(2):

            def go():
                a_half(ev, z, parity).wait_send()
                a_twin(0, twin, z, parity).wait_recv()
                a_twin(1, twin_half, z, parity).wait_recv()
                a_twin(0, ev, z, parity).wait_send()
                a_twin(1, half, z, parity).wait_send()
                if early:
                    for side in range(2):
                        b_twin(side, (twin, twin_half)[side], z, parity).wait_recv()
                        b_twin(side, (ev, half)[side], z, parity).wait_send()

            when_owner(device(z, parity), go)

    if early:
        b_half(ev).wait_send()


def body(
    n,
    n_event,
    reach_attrs,
    w_first,
    b_first,
    w_second,
    b_second,
    w_out,
    section_factor,
    bed_slope,
    seg_count,
    section_class,
    down_local,
    send_list,
    recv_list,
    area_start,
    lateral,
    cotangent,
):
    f32, bf16 = jnp.float32, jnp.bfloat16
    events, reaches = area_start.shape
    feat, hid = w_first.shape
    class_total = section_factor.shape[0]
    part = hid // n_event
    owners = n if part % (8 * n) == 0 else part // 8
    chunk = part // owners
    scale = 32.0 / math.sqrt(events * n_event * reaches * n)
    one_hot = (section_class[None, :] == jnp.arange(class_total, dtype=jnp.int32)[:, None]).astype(f32)
    k_base = jnp.sqrt(bed_slope) * jnp.sum(one_hot * section_factor[:, None], axis=0)
    position = jnp.arange(reaches, dtype=jnp.int32)
    hop = jnp.where(down_local < reaches, down_local - position, 0).astype(f32)
    rows = jnp.stack([k_base, 1.0 / seg_count.astype(f32), hop], axis=0)
    cols = jnp.stack([b_first, b_second, w_out.astype(f32)], axis=1)
    attrs = jnp.concatenate(
        [reach_attrs.T, jnp.ones((1, reaches), bf16), jnp.zeros((127 - feat, reaches), bf16)], axis=0
    )
    vmem = pl.BlockSpec(memory_space=pltpu.VMEM)
    dma = pltpu.SemaphoreType.DMA
    wide = hid + 128
    outflow, grad_lateral, full = pl.pallas_call(
        functools.partial(kernel, n, n_event, owners, chunk, scale),
        out_shape=(
            jax.ShapeDtypeStruct((events, reaches), f32),
            jax.ShapeDtypeStruct((STEPS, events, reaches), f32),
            jax.ShapeDtypeStruct((hid, wide), f32),
        ),
        in_specs=[vmem] * 11,
        out_specs=(vmem,) * 3,
        scratch_shapes=[
            pltpu.VMEM((hid, reaches), f32),
            pltpu.VMEM((hid, reaches), bf16),
            pltpu.VMEM((hid, reaches), f32),
            pltpu.VMEM((hid, reaches), bf16),
            pltpu.VMEM((hid, reaches), bf16),
            pltpu.VMEM((1, reaches), f32),
            pltpu.VMEM((LINKS * GROUP, reaches), bf16),
            pltpu.VMEM((LINKS * GROUP, reaches), bf16),
            pltpu.VMEM((2 * STEPS, LINKS, 8, 128), f32),
            pltpu.VMEM((2 * STEPS, LINKS, 8, 128), f32),
            pltpu.VMEM((1, reaches), f32),
            pltpu.VMEM((n_event - 1, 1, reaches), f32),
            pltpu.VMEM((part, wide), f32),
            pltpu.VMEM((n // 2, chunk, wide), f32),
            pltpu.VMEM((n // 2, chunk, wide), f32),
            dma((2 * STEPS, LINKS)),
            dma((2 * STEPS, LINKS)),
            dma((n_event - 1,)),
            dma((n_event - 1,)),
            dma((n // 2,)),
            dma((n // 2,)),
            dma((n // 2,)),
            dma((n // 2,)),
            dma((n // 2,)),
            dma((n // 2,)),
            dma((n // 2,)),
            dma((n // 2,)),
            dma((n,)),
            dma((n,)),
            dma((2, n)),
            dma((2, n)),
            dma((2, n // 2)),
            dma((2, n // 2)),
            dma((2, n // 2)),
            dma((2, n // 2)),
            dma,
            dma,
            dma((2, n)),
            dma((2, n)),
        ],
        compiler_params=pltpu.CompilerParams(
            collective_id=0, has_side_effects=True, vmem_limit_bytes=48 * 1024 * 1024
        ),
    )(
        w_first.T, w_second, w_second.T, cols, attrs, rows, send_list, recv_list,
        area_start, lateral, cotangent,
    )
    small = full[:, hid : hid + feat + 3].T
    return (
        outflow,
        grad_lateral,
        small[:feat],
        small[feat],
        full[:, :hid],
        small[feat + 1],
        small[feat + 2],
    )


def solution(mesh):
    return jax.shard_map(
        functools.partial(body, mesh.shape["basin"], mesh.shape["event"]),
        mesh=mesh,
        in_specs=(
            P("basin", None),
            P(),
            P(),
            P(),
            P(),
            P(),
            P(),
            P("basin"),
            P("basin"),
            P("basin"),
            P("basin"),
            P("basin", None, None),
            P("basin", None, None),
            P("event", "basin"),
            P(None, "event", "basin"),
            P("event", "basin"),
        ),
        out_specs=(P("event", "basin"), P(None, "event", "basin"), P(), P(), P(), P(), P()),
        check_vma=False,
    )
```

profile of v0, /device:TPU:9, one launch (start us, length us, event | category | flops | bytes accessed | tf_op | source)
XLA Modules:
  0.0 97.1 jit_solution(17068427573008819833)
XLA Ops:
  0.6 0.0 copy-start
  0.6 0.0 copy-start.14
  0.7 0.0 copy-start.12
  0.7 0.0 copy-start.13
  0.7 0.0 copy-start.10
  0.7 0.0 copy-start.11
  0.7 0.0 copy-start.8
  0.7 0.0 copy-start.9
  0.7 0.0 copy-start.4
  0.7 1.7 %copy.37 = bf16[768,768]{0,1:T(8,128)(2,1)S(1)} copy(bf16[768,768]{1,0:T(8,128)(2,1)} %w_second.1) | data formatting | bytes 2359296 | tf_op args[3]
  2.4 0.0 copy-done.14
  2.4 0.0 copy-done.12
  2.5 0.0 copy-done.13
  2.5 0.2 copy.38.cols
  2.7 0.1 pad.5.clone
  2.8 0.1 pad.4.clone
  2.9 0.0 copy-done.10
  2.9 0.1 maximum_maximum_fusion.attrs
  3.0 1.0 copy.36
  3.9 0.8 select_reduce_fusion
  4.8 0.0 copy-done.11
  4.8 0.7 convert_divide_fusion
  5.5 0.7 select_convert_fusion
  6.3 0.0 copy-done
  6.3 0.0 copy-done.8
  6.3 0.0 copy-done.9
  6.3 0.0 copy-done.4
  6.3 0.0 copy-start.3
  6.3 1.1 %copy-done.3 = f32[3,32,1536]{2,1,0:T(8,128)S(1)} copy-done((f32[3,32,1536]{2,1,0:T(8,128)S(1)}, f32[3,32,1536]{2,1,0:T(8,128)}, u32[]{:S(2)}) %copy-start.3) | copy-done | bytes 589848
  7.4 0.0 copy-start.5
  7.4 0.9 copy-done.5
  8.3 79.4 %shard_map.207 = (f32[32,1536]{1,0:T(8,128)S(1)}, f32[3,32,1536]{2,1,0:T(8,128)S(1)}, f32[768,896]{1,0:T(8,128)}) custom-call(bf16[768,32]{1,0:T(8,128)(2,1)S(1)} %bitcast.8, bf16[768,768]{1,0:T(8,128)(2,1)S(1)} %copy-done, bf16[768,768]{1,0:T(8,128)(2,1)S(1)} %bitcast.7, f32[768,3]{1,0:T(8,128)S(1)} %copy.38.cols, ...), custom_call_target="tpu_custom_call" | custom-call | tf_op jit(solution)/shard_map/pallas_call | solution.py:504
  87.7 0.0 copy-start.1
  87.7 0.8 copy-done.1
  88.5 0.0 copy-start.6
  88.5 0.7 copy-done.6
  89.2 1.0 %slice_bitcast_fusion = f32[35,768]{0,1:T(8,128)S(1)} fusion(f32[768,896]{1,0:T(8,128)} %get-tuple-element.12), kind=kLoop, calls=%fused_computation.4 | loop fusion | bytes 215040 | tf_op jit(solution)/shard_map/transpose | solution.py:561
  90.2 1.3 %slice_reduce_fusion = (f32[768]{0:T(1024)}, f32[768]{0:T(1024)}, f32[768]{0:T(1024)}) fusion(f32[35,768]{0,1:T(8,128)S(1)} %slice_bitcast_fusion), kind=kLoop, calls=%fused_computation | loop fusion | bytes 18432 | tf_op jit(solution)/shard_map/slice | solution.py:569
  91.5 0.8 copy.39
  92.3 0.0 copy-start.7
  92.3 0.0 copy-start.2
  92.3 3.3 %slice.21 = f32[768,768]{1,0:T(8,128)} slice(f32[768,896]{1,0:T(8,128)} %get-tuple-element.12), slice={[0:768], [0:768]} | slice | bytes 4718592 | tf_op jit(solution)/shard_map/slice | solution.py:567
  95.6 0.0 copy-done.7
  95.6 0.7 copy.42
  96.3 0.0 copy-done.2
  96.3 0.8 copy.43
  (10 shorter events, 0.1 us)
Async XLA Ops:
  0.6 5.6 %copy-start = (bf16[768,768]{1,0:T(8,128)(2,1)S(1)}, bf16[768,768]{1,0:T(8,128)(2,1)}, u32[]{:S(2)}) copy-start(bf16[768,768]{1,0:T(8,128)(2,1)} %w_second.1) | copy-start | bytes 3538948
  0.6 1.8 %copy-start.14 = (bf16[768]{0:T(1024)(128)(2,1)S(1)}, bf16[768]{0:T(1024)(128)(2,1)}, u32[]{:S(2)}) copy-start(bf16[768]{0:T(1024)(128)(2,1)} %param.21) | copy-start | bytes 4612
  0.7 1.8 %copy-start.12 = (f32[768]{0:T(1024)S(1)}, f32[768]{0:T(1024)}, u32[]{:S(2)}) copy-start(f32[768]{0:T(1024)} %param.18) | copy-start | bytes 9220
  0.7 1.8 %copy-start.13 = (f32[768]{0:T(1024)S(1)}, f32[768]{0:T(1024)}, u32[]{:S(2)}) copy-start(f32[768]{0:T(1024)} %param.20) | copy-start | bytes 9220
  0.7 2.2 %copy-start.10 = (bf16[1536,32]{0,1:T(8,128)(2,1)S(1)}, bf16[1536,32]{0,1:T(8,128)(2,1)}, u32[]{:S(2)}) copy-start(bf16[1536,32]{0,1:T(8,128)(2,1)} %param.16) | copy-start | bytes 294916
  0.7 4.1 %copy-start.11 = (f32[1536]{0:T(1024)S(1)}, f32[1536]{0:T(1024)}, u32[]{:S(2)}) copy-start(f32[1536]{0:T(1024)} %param.23) | copy-start | bytes 18436
  0.7 5.6 %copy-start.8 = (s32[1,8,24]{2,1,0:T(8,128)S(1)}, s32[1,8,24]{2,1,0:T(8,128)}, u32[]{:S(2)}) copy-start(s32[1,8,24]{2,1,0:T(8,128)} %send_list.1) | copy-start | bytes 2308
  0.7 5.6 %copy-start.9 = (s32[1,8,24]{2,1,0:T(8,128)S(1)}, s32[1,8,24]{2,1,0:T(8,128)}, u32[]{:S(2)}) copy-start(s32[1,8,24]{2,1,0:T(8,128)} %recv_list.1) | copy-start | bytes 2308
  0.7 5.6 %copy-start.4 = (f32[32,1536]{1,0:T(8,128)S(1)}, f32[32,1536]{1,0:T(8,128)}, u32[]{:S(2)}) copy-start(f32[32,1536]{1,0:T(8,128)} %area_start.1) | copy-start | bytes 589828
  6.3 1.1 %copy-start.3 = (f32[3,32,1536]{2,1,0:T(8,128)S(1)}, f32[3,32,1536]{2,1,0:T(8,128)}, u32[]{:S(2)}) copy-start(f32[3,32,1536]{2,1,0:T(8,128)} %lateral.1) | copy-start | bytes 1769476
  7.4 0.9 copy-start.5
  87.7 0.8 copy-start.1
  88.5 0.7 copy-start.6
  92.3 3.3 %copy-start.7 = (f32[32,1536]{1,0:T(8,128)S(1)}, f32[32,1536]{1,0:T(8,128)}, u32[]{:S(2)}) copy-start(f32[32,1536]{1,0:T(8,128)} %copy-done.6) | copy-start | bytes 589828
  92.3 4.0 %copy-start.2 = (f32[3,32,1536]{2,1,0:T(8,128)S(1)}, f32[3,32,1536]{2,1,0:T(8,128)}, u32[]{:S(2)}) copy-start(f32[3,32,1536]{2,1,0:T(8,128)} %copy-done.1) | copy-start | bytes 1769476
where the time goes:
time: 98.7 us; the launch traced here: 97.1 us
  Pallas kernels  79.4 us (80%)
  local copies, waits for them, and re-layouts  14.4 us (15%)
  other arithmetic  2.37 us (2%)
    pallas_call x1, Pallas kernels, body(): pl.pallas_call(functools.partial(kernel, n, n_event, owners, chunk, scale...  79.4 us
    unnamed x35, local copies, waits for them, and re-layouts  8.44 us
    slice x1, local copies, waits for them, and re-layouts, body(): full[:, :hid]  3.29 us

commit v1 on v0

v1 whole, which is shorter than its diff:
```python
import functools
import math

import jax
import jax.numpy as jnp
from jax import lax
from jax.experimental import pallas as pl
from jax.experimental.pallas import tpu as pltpu
from jax.sharding import PartitionSpec as P

STEPS = 3
LINKS = 4
GROUP = 32
PLACES = 48
MESH = pl.DeviceIdType.MESH
NT = (((1,), (1,)), ((), ()))


def split_two(x):
    high = x.astype(jnp.bfloat16)
    low = (x - high.astype(jnp.float32)).astype(jnp.bfloat16)
    return jnp.concatenate([high, low], axis=0)


def kernel(
    n, n_event, owners, chunk, scale,
    attrs_h, w_first_h, b_first_h, w_second_h, b_second_h, w_out_h, section_factor,
    bed_slope_h, seg_count_h, section_class_h, down_local_h, send_list_h, recv_list_h,
    area_start_h, lateral_h, cotangent_h,
    outflow, grad_lateral, full,
    attrs, w_first, b_first, w_second, b_second, w_out,
    bed_slope, seg_count, section_class, down_local, send_list, recv_list,
    area_start, lateral, cotangent, load_sem,
    w_firstT, w_secondT, cols,
    t_one, h_one, d_two, h_two, lower, squash_all, take_send, take_recv,
    out_msg, in_msg, rate_out, rate_in, slab, rs_pair, rs_line,
    s_send, s_recv,
    x_send, x_recv, r_send, r_recv, px_send, px_recv, pz_send, pz_recv,
    az_send, az_recv, ax_send, ax_recv, ay_send, ay_recv,
    fa_send, fa_recv, fb_send, fb_recv, tw_send, tw_recv,
):
    f32, bf16 = jnp.float32, jnp.bfloat16
    me = lax.axis_index("basin")
    ev = lax.axis_index("event")
    events, reaches = area_start.shape
    hid = w_second.shape[0]
    feat = w_first.shape[0]
    part = hid // n_event
    offsets = (1, 2, n // 2, n - 1)
    base = pl.multiple_of(ev * part, 64)
    mine = pl.ds(base, part)
    width = reaches // n_event

    loads = {}
    for name, source, target in (
        ("w_first", w_first_h, w_first),
        ("attrs", attrs_h, attrs.at[pl.ds(0, feat)]),
        ("b_first", b_first_h, b_first),
        ("b_second", b_second_h, b_second),
        ("w_out", w_out_h, w_out),
        ("w_second", w_second_h, w_second),
        ("send_list", send_list_h, send_list),
        ("recv_list", recv_list_h, recv_list),
        ("bed_slope", bed_slope_h, bed_slope),
        ("section_class", section_class_h, section_class),
        ("seg_count", seg_count_h, seg_count),
        ("down_local", down_local_h, down_local),
        ("area_start", area_start_h, area_start),
        ("lateral", lateral_h, lateral),
        ("cotangent", cotangent_h, cotangent),
    ):
        loads[name] = pltpu.make_async_copy(source, target, load_sem.at[len(loads)])
        loads[name].start()

    barrier = pltpu.get_barrier_semaphore()

    @pl.loop(1, n)
    def _(i):
        pl.semaphore_signal(barrier, inc=1, device_id={"basin": lax.rem(me + i, n)}, device_id_type=MESH)

    for i in range(1, n_event):
        pl.semaphore_signal(
            barrier, inc=1, device_id={"event": lax.rem(ev + i, n_event)}, device_id_type=MESH
        )

    for name in ("w_first", "attrs", "b_first", "b_second", "w_out", "w_second"):
        loads[name].wait()

    extra = attrs.shape[0] - feat
    attrs[feat:, :] = jnp.where(
        lax.broadcasted_iota(jnp.int32, (extra, reaches), 0) == 0, 1.0, 0.0
    ).astype(bf16)
    w_firstT[...] = jnp.transpose(w_first[...])
    w_secondT[...] = jnp.transpose(w_second[...])
    w_out_row = w_out[...].astype(f32).reshape(1, hid)
    cols[...] = jnp.transpose(jnp.concatenate(
        [b_first[...].reshape(1, hid), b_second[...].reshape(1, hid), w_out_row,
         jnp.zeros((5, hid), f32)], axis=0
    ))
    w_out_rows = jnp.broadcast_to(w_out_row, (16, hid)).astype(bf16)

    def network(block):
        where = pl.ds(pl.multiple_of(block * width, 128), width)
        one = jnp.tanh(
            jnp.dot(w_firstT[...], attrs[0:feat, where], preferred_element_type=f32) + cols[:, 0:1]
        )
        t_one[:, where] = one
        hidden = one.astype(bf16)
        h_one[:, where] = hidden
        two = jnp.tanh(
            jnp.dot(w_secondT[...], hidden, preferred_element_type=f32) + cols[:, 1:2]
        )
        rounded = two.astype(bf16)
        h_two[:, where] = rounded
        factor = (cols[:, 2:3] * (1.0 - two * two)).astype(bf16)
        d_two[:, where] = factor
        first = t_one[mine, where]
        lower[:, where] = (
            jnp.dot(w_second[mine, :], factor, preferred_element_type=f32) * (1.0 - first * first)
        )
        return rounded

    logit = jnp.dot(w_out_rows, network(ev), preferred_element_type=f32)[0:1]
    squash_all[ev] = 1.0 / (1.0 + jnp.exp(-logit))

    pl.semaphore_wait(barrier, n - 1 + n_event - 1)

    def squash_copy(i):
        return pltpu.make_async_remote_copy(
            src_ref=squash_all.at[ev],
            dst_ref=squash_all.at[ev],
            send_sem=s_send.at[i],
            recv_sem=s_recv.at[i],
            device_id={"event": lax.rem(ev + 1 + i, n_event)},
            device_id_type=MESH,
        )

    for i in range(n_event - 1):
        squash_copy(i).start()

    for name in ("send_list", "recv_list", "bed_slope", "section_class", "seg_count", "down_local",
                 "area_start"):
        loads[name].wait()

    slot_row = lax.broadcasted_iota(jnp.int32, (LINKS * GROUP, 1), 0)
    slot = slot_row % GROUP
    cap = send_list.shape[2]
    spread = (
        slot == lax.broadcasted_iota(jnp.int32, (LINKS * GROUP, cap), 1)
    ).astype(f32)
    lane_reach = lax.broadcasted_iota(jnp.int32, (LINKS * GROUP, reaches), 1).astype(f32)
    lane_basin = lax.broadcasted_iota(jnp.int32, (LINKS * GROUP, n), 1)

    def one_hot_of(lists, sign):
        table = lax.dot_general(
            spread, lists[0].astype(f32), NT, precision=lax.Precision.HIGHEST,
            preferred_element_type=f32,
        )
        peer = jnp.zeros((LINKS * GROUP, 1), jnp.int32)
        for k, off in enumerate(offsets):
            peer = jnp.where(slot_row // GROUP == k, lax.rem(me + sign * off + n, n), peer)
        column = jnp.sum(jnp.where(lane_basin == peer, table, 0.0), axis=1, keepdims=True)
        column = jnp.where(slot < cap, column, float(reaches))
        return (jnp.abs(lane_reach - column) < 0.5).astype(bf16)

    take_send[...] = one_hot_of(send_list, 1)
    take_recv[...] = one_hot_of(recv_list, -1)

    kind = section_class[...].reshape(1, reaches)
    conveyance = jnp.zeros((1, reaches), f32)
    for c in range(section_factor.shape[0]):
        conveyance = jnp.where(kind == c, section_factor[c], conveyance)
    k_base = jnp.sqrt(bed_slope[...].reshape(1, reaches)) * conveyance
    beta = 1.0 / seg_count[...].reshape(1, reaches).astype(f32)
    down = down_local[...].reshape(1, reaches)
    hop = jnp.where(down < reaches, down - lax.broadcasted_iota(jnp.int32, (1, reaches), 1), 0)
    masks = [(hop == d).astype(f32) for d in range(1, 9)]

    network(lax.rem(ev + 1, n_event))

    for i in range(n_event - 1):
        squash_copy(i).wait_recv()
    squash = jnp.concatenate([squash_all[e] for e in range(n_event)], axis=1)
    rough = 0.02 + 0.08 * squash
    rate = k_base / rough
    lane_group = lax.broadcasted_iota(jnp.int32, (8, 128), 1) // GROUP
    blocks = events // 8

    def message(index, k, sign):
        return pltpu.make_async_remote_copy(
            src_ref=out_msg.at[index, k],
            dst_ref=in_msg.at[index, k],
            send_sem=x_send.at[index, k],
            recv_sem=x_recv.at[index, k],
            device_id={"basin": lax.rem(me + sign * offsets[k] + n, n)},
            device_id_type=MESH,
        )

    def send(index, field, matrix, sign):
        both = lax.dot_general(split_two(field), matrix[...], NT, preferred_element_type=f32)
        picked = both[:events] + both[events:]
        for k in range(LINKS):
            packed = jnp.zeros((8, 128), f32)
            for q in range(blocks):
                piece = picked[8 * q : 8 * q + 8]
                shift = ((q - k) * GROUP) % 128
                if shift:
                    piece = pltpu.roll(piece, shift, 1)
                packed = jnp.where(lane_group == q, piece, packed)
            out_msg[index, k] = packed
            message(index, k, sign).start()

    def receive(index, matrix, sign):
        for k in range(LINKS):
            message(index, k, sign).wait_recv()
        pieces = []
        for q in range(blocks):
            got = jnp.zeros((8, 128), f32)
            for k in range(LINKS):
                piece = in_msg[index, k]
                shift = ((k - q) * GROUP) % 128
                if shift:
                    piece = pltpu.roll(piece, shift, 1)
                got = jnp.where(lane_group == k, piece, got)
            pieces.append(got)
        both = jnp.dot(
            split_two(jnp.concatenate(pieces, axis=0)), matrix[...], preferred_element_type=f32
        )
        return both[:events] + both[events:]

    def power(area):
        return jnp.exp((2.0 / 3.0) * jnp.log(area))

    areas = [area_start[...]]
    powers = [power(areas[0])]
    shrinks = []
    for t in range(STEPS):
        area, p = areas[t], powers[t]
        flow = rate * area * p
        send(t, flow, take_send, 1)
        if t == 0:
            loads["lateral"].wait()
        inflow = lateral[t]
        for d in range(1, 9):
            inflow = inflow + pltpu.roll(flow * masks[d - 1], d, 1)
        shrink = 1.0 / (1.0 + beta * rate * p)
        shrinks.append(shrink)
        if t < n_event - 2:
            network(lax.rem(ev + 2 + t, n_event))
        inflow = inflow + receive(t, take_recv, 1)
        areas.append((area + beta * inflow) * shrink)
        powers.append(power(areas[t + 1]))
    emitted = areas[STEPS] * powers[STEPS]
    outflow[...] = rate * emitted
    loads["cotangent"].wait()
    g_area = cotangent[...] * rate * (5.0 / 3.0) * powers[STEPS]
    g_rate = cotangent[...] * emitted
    for t in reversed(range(STEPS)):
        index = 2 * STEPS - 1 - t
        inner = g_area * shrinks[t]
        g_inflow = inner * beta
        grad_lateral[t] = g_inflow
        send(index, g_inflow, take_recv, -1)
        g_flow = jnp.zeros((events, reaches), f32)
        for d in range(1, 9):
            g_flow = g_flow + masks[d - 1] * pltpu.roll(g_inflow, reaches - d, 1)
        drop = g_inflow * areas[t + 1] * powers[t]
        g_rate = g_rate - drop
        g_area = inner - (2.0 / 3.0) * rate * drop / areas[t]
        g_flow = g_flow + receive(index, take_send, -1)
        g_rate = g_rate + g_flow * areas[t] * powers[t]
        g_area = g_area + (5.0 / 3.0) * rate * powers[t] * g_flow
    rate_out[...] = jnp.sum(g_rate, axis=0, keepdims=True)

    def rate_copy(i):
        return pltpu.make_async_remote_copy(
            src_ref=rate_out,
            dst_ref=rate_in.at[i],
            send_sem=r_send.at[i],
            recv_sem=r_recv.at[i],
            device_id={"event": lax.rem(ev + 1 + i, n_event)},
            device_id_type=MESH,
        )

    for i in range(n_event - 1):
        rate_copy(i).start()
    for i in range(n_event - 1):
        rate_copy(i).wait_recv()
    terms = [rate_out[...]] + [rate_in[i] for i in range(n_event - 1)]
    g_sum = jnp.zeros((1, reaches), f32)
    for e in range(n_event):
        term = terms[0]
        for i in range(n_event - 1):
            term = jnp.where(lax.rem(e + 1 + i, n_event) == ev, terms[i + 1], term)
        g_sum = g_sum + term
    g_logit = (
        g_sum * (-rate / rough) * (scale * 0.08) * squash * (1.0 - squash)
    ).astype(bf16)
    g_logit32 = g_logit.astype(f32)

    scaled = (h_one[mine, :].astype(f32) * g_logit32).astype(bf16)
    large = lax.dot_general(scaled, d_two[...], NT, preferred_element_type=f32)
    tiles = hid // 128
    for d in range(owners):
        for r in range(chunk // 8):
            for c in range(tiles):
                top = d * chunk + 8 * r
                slab[d, r * tiles + c] = large[top : top + 8, 128 * c : 128 * c + 128]

    g_pre = (lower[...] * g_logit32).astype(bf16)
    place = lax.broadcasted_iota(jnp.int32, (PLACES, reaches), 0)
    row_two = jnp.where(place == feat + 1, g_logit32, 0.0).astype(bf16)
    row_out = jnp.where(place == feat + 2, g_logit32, 0.0).astype(bf16)
    g_two = d_two[mine, :]
    second = h_two[mine, :]

    def narrow(low):
        high = low + 128
        return (
            lax.dot_general(attrs[...], g_pre[low:high], NT, preferred_element_type=f32)
            + lax.dot_general(row_two, g_two[low:high], NT, preferred_element_type=f32)
            + lax.dot_general(row_out, second[low:high], NT, preferred_element_type=f32)
        )

    left = narrow(0)
    right = narrow(part - 128)
    first_half = lax.broadcasted_iota(jnp.int32, (8, 128), 1) < 64
    last = slab.shape[1] - 1
    for k in range(5):
        slab[k, last] = left[8 * k : 8 * k + 8]
    for k in range(3):
        even = pltpu.roll(right[16 * k : 16 * k + 8], 64, 1)
        slab[5 + k, last] = jnp.where(first_half, even, right[16 * k + 8 : 16 * k + 16])
    for d in range(8, owners):
        slab[d, last] = jnp.zeros((8, 128), f32)

    def when_owner(index, work):
        if owners == n:
            work()
        else:
            pl.when(index < owners)(work)

    line = n // 2
    low = lax.rem(me, 2)
    spot = me // 2
    pair = me + 1 - 2 * low
    half = lax.rem(ev + n_event // 2, n_event)
    twin = ev + 1 - 2 * lax.rem(ev, 2)
    twin_half = lax.rem(twin + n_event // 2, n_event)
    span = slab.shape[1]
    cut = (span + 1) // 2

    def each(first, last, work):
        if last - first <= 4:
            for j in range(first, last):
                work(j)
        else:
            pl.loop(first, last)(work)

    def near(j):
        if line != 4:
            return lax.rem(spot + j, line)
        if isinstance(j, int) and j == 0:
            return spot
        orders = ((1, 2, 3), (2, 0, 3), (1, 3, 0), (2, 1, 0))
        code = sum(orders[s][j - 1] * 4 ** s for s in range(4))
        power_of = (1 + 3 * lax.rem(spot, 2)) * (1 + 15 * (spot // 2))
        return lax.rem(code // power_of, 4)

    def device(z, parity):
        return 2 * z + parity

    def pair_sum(z, parity):
        return pltpu.make_async_remote_copy(
            src_ref=slab.at[device(z, parity)], dst_ref=rs_pair.at[z],
            send_sem=px_send.at[z], recv_sem=px_recv.at[z],
            device_id={"basin": pair}, device_id_type=MESH,
        )

    def line_sum(z, sender):
        return pltpu.make_async_remote_copy(
            src_ref=rs_pair.at[z], dst_ref=rs_line.at[sender],
            send_sem=pz_send.at[z], recv_sem=pz_recv.at[sender],
            device_id={"basin": device(z, low)}, device_id_type=MESH,
        )

    def far(j):
        return near(line - 1 - j)

    def start_pair(j):
        z = far(j)
        when_owner(device(z, 1 - low), lambda: pair_sum(z, 1 - low).start())

    each(0, line, start_pair)

    def add_pair(j):
        z = far(j)

        def go():
            pair_sum(z, 1 - low).wait_recv()
            rs_pair[z] = rs_pair[z] + slab[device(z, low)]

            @pl.when(z != spot)
            def _():
                line_sum(z, spot).start()

        when_owner(device(z, low), go)

    each(0, line, add_pair)

    whole = pl.ds(0, span)
    upper = pl.ds(0, cut)
    under = pl.ds(cut, span - cut)

    def move(event, at, rows, sems, slot, target):
        ref = full.at[event, at, rows]
        return pltpu.make_async_remote_copy(
            src_ref=ref, dst_ref=ref, send_sem=sems[0].at[slot], recv_sem=sems[1].at[slot],
            device_id=target, device_id_type=MESH,
        )

    def to_line(source, peer):
        ref = full.at[ev, device(source, low)]
        return pltpu.make_async_remote_copy(
            src_ref=ref, dst_ref=ref, send_sem=az_send.at[peer], recv_sem=az_recv.at[source],
            device_id={"basin": device(peer, low)}, device_id_type=MESH,
        )

    def to_pair(z, parity):
        return move(ev, device(z, parity), whole, (ax_send, ax_recv), z, {"basin": pair})

    def to_half(event, z):
        return move(event, device(z, low), whole, (ay_send, ay_recv), z, {"event": half})

    def on_half(event, z):
        return move(event, device(z, 1 - low), upper, (fa_send, fa_recv), z, {"event": half})

    def on_pair(z, parity):
        return move(half, device(z, parity), under, (fb_send, fb_recv), z, {"basin": pair})

    def to_twin(side, event, z):
        ref = full.at[event, pl.ds(2 * z, 2)]
        return pltpu.make_async_remote_copy(
            src_ref=ref, dst_ref=ref, send_sem=tw_send.at[side, z], recv_sem=tw_recv.at[side, z],
            device_id={"event": twin}, device_id_type=MESH,
        )

    def own():
        def add(i, total):
            sender = lax.rem(spot + line - i, line)
            line_sum(spot, sender).wait_recv()
            return total + rs_line[sender]

        full[ev, me] = lax.fori_loop(1, line, add, rs_pair[spot])
        each(1, line, lambda j: to_line(spot, near(j)).start())
        to_pair(spot, low).start()
        to_half(ev, spot).start()

    when_owner(me, own)

    def from_line(j):
        z = near(j)

        def go():
            to_line(z, spot).wait_recv()
            to_pair(z, low).start()
            to_half(ev, z).start()

        when_owner(device(z, low), go)

    def second_hop(j):
        z = near(j)

        def go():
            to_pair(z, 1 - low).wait_recv()
            on_half(ev, z).start()
            to_twin(0, ev, z).start()
            to_half(half, z).wait_recv()
            on_pair(z, low).start()

        when_owner(2 * z, go)

    def corner(j):
        z = near(j)

        def go():
            on_half(half, z).wait_recv()
            on_pair(z, 1 - low).wait_recv()
            to_twin(1, half, z).start()

        when_owner(2 * z, go)

    if line <= 4:
        for j in range(1, line):
            from_line(j)
            second_hop(j - 1)
            if j >= 2:
                corner(j - 2)
        second_hop(line - 1)
        corner(line - 2)
        corner(line - 1)
    else:
        pl.loop(1, line)(from_line)
        pl.loop(0, line)(second_hop)
        pl.loop(0, line)(corner)

    for i in range(n_event - 1):
        squash_copy(i).wait_send()
    for index in range(2 * STEPS):
        for k in range(LINKS):
            message(index, k, 1).wait_send()
    for i in range(n_event - 1):
        rate_copy(i).wait_send()

    def drain(z):
        when_owner(device(z, 1 - low), lambda: pair_sum(z, 1 - low).wait_send())

        @pl.when(z != spot)
        def _():
            when_owner(device(z, low), lambda: line_sum(z, spot).wait_send())
            when_owner(me, lambda: to_line(spot, z).wait_send())

        def go():
            to_pair(z, low).wait_send()
            to_half(ev, z).wait_send()
            on_half(ev, z).wait_send()
            on_pair(z, low).wait_send()
            to_twin(0, ev, z).wait_send()
            to_twin(1, half, z).wait_send()

        when_owner(2 * z, go)

    each(0, line, drain)

    def arrive(j):
        z = near(j)

        def go():
            to_twin(0, twin, z).wait_recv()
            to_twin(1, twin_half, z).wait_recv()

        when_owner(2 * z, go)

    each(0, line, arrive)


def finish(
    feat, full, flow_in, lateral_in,
    large, flow_out, lateral_out, w_first, b_first, b_second, w_out, sems,
):
    last = full.shape[2] - 1
    copies = [
        pltpu.make_async_copy(full.at[:, :, pl.ds(0, last)], large, sems.at[0]),
        pltpu.make_async_copy(lateral_in, lateral_out, sems.at[1]),
        pltpu.make_async_copy(flow_in, flow_out, sems.at[2]),
    ]
    for copy in copies:
        copy.start()
    n_event = full.shape[0]
    first_half = lax.broadcasted_iota(jnp.int32, (8, 128), 1) < 64
    for k in range(5):
        columns = []
        for e in range(0, n_event, 2):
            tails = []
            for s in range(2):
                tail = full[e + s, 5 + k // 2, last]
                tails.append(pltpu.roll(tail, 64, 1) if k % 2 != s else tail)
            turned = pltpu.roll(full[e + 1, k, last], 64, 1)
            columns += [
                full[e, k, last],
                jnp.where(first_half, tails[0], turned),
                jnp.where(first_half, turned, tails[1]),
            ]
        rows = jnp.concatenate(columns, axis=1)
        if k < 4:
            w_first[8 * k : 8 * k + 8, :] = rows
        else:
            b_first[...] = rows[0:1].reshape(rows.shape[1])
            b_second[...] = rows[1:2].reshape(rows.shape[1])
            w_out[...] = rows[2:3].reshape(rows.shape[1])
    for copy in copies:
        copy.wait()


def body(
    n,
    n_event,
    reach_attrs,
    w_first,
    b_first,
    w_second,
    b_second,
    w_out,
    section_factor,
    bed_slope,
    seg_count,
    section_class,
    down_local,
    send_list,
    recv_list,
    area_start,
    lateral,
    cotangent,
):
    f32, bf16 = jnp.float32, jnp.bfloat16
    events, reaches = area_start.shape
    feat, hid = w_first.shape
    part = hid // n_event
    owners = n if part % (8 * n) == 0 else part // 8
    chunk = part // owners
    span = (chunk // 8) * (hid // 128) + 1
    line = n // 2
    scale = 32.0 / math.sqrt(events * n_event * reaches * n)
    vmem = pl.BlockSpec(memory_space=pltpu.VMEM)
    hbm = pl.BlockSpec(memory_space=pltpu.HBM)
    smem = pl.BlockSpec(memory_space=pltpu.SMEM)
    dma = pltpu.SemaphoreType.DMA
    held = lambda x: pltpu.VMEM(x.shape, x.dtype)
    outflow, grad_lateral, full = pl.pallas_call(
        functools.partial(kernel, n, n_event, owners, chunk, scale),
        out_shape=(
            jax.ShapeDtypeStruct((events, reaches), f32),
            jax.ShapeDtypeStruct((STEPS, events, reaches), f32),
            jax.ShapeDtypeStruct((n_event, owners, span, 8, 128), f32),
        ),
        in_specs=[hbm] * 6 + [smem] + [hbm] * 9,
        out_specs=(vmem,) * 3,
        scratch_shapes=[
            pltpu.VMEM((PLACES, reaches), bf16),
            held(w_first), held(b_first), held(w_second), held(b_second), held(w_out),
            held(bed_slope), held(seg_count), held(section_class), held(down_local),
            held(send_list), held(recv_list), held(area_start), held(lateral), held(cotangent),
            dma((15,)),
            pltpu.VMEM((hid, feat), bf16),
            pltpu.VMEM((hid, hid), bf16),
            pltpu.VMEM((hid, 8), f32),
            pltpu.VMEM((hid, reaches), f32),
            pltpu.VMEM((hid, reaches), bf16),
            pltpu.VMEM((hid, reaches), bf16),
            pltpu.VMEM((hid, reaches), bf16),
            pltpu.VMEM((part, reaches), f32),
            pltpu.VMEM((n_event, 1, reaches // n_event), f32),
            pltpu.VMEM((LINKS * GROUP, reaches), bf16),
            pltpu.VMEM((LINKS * GROUP, reaches), bf16),
            pltpu.VMEM((2 * STEPS, LINKS, 8, 128), f32),
            pltpu.VMEM((2 * STEPS, LINKS, 8, 128), f32),
            pltpu.VMEM((1, reaches), f32),
            pltpu.VMEM((n_event - 1, 1, reaches), f32),
            pltpu.VMEM((owners, span, 8, 128), f32),
            pltpu.VMEM((line, span, 8, 128), f32),
            pltpu.VMEM((line, span, 8, 128), f32),
            dma((n_event - 1,)), dma((n_event - 1,)),
            dma((2 * STEPS, LINKS)), dma((2 * STEPS, LINKS)),
            dma((n_event - 1,)), dma((n_event - 1,)),
            dma((line,)), dma((line,)), dma((line,)), dma((line,)),
            dma((line,)), dma((line,)), dma((line,)), dma((line,)), dma((line,)), dma((line,)),
            dma((line,)), dma((line,)), dma((line,)), dma((line,)), dma((2, line)), dma((2, line)),
        ],
        compiler_params=pltpu.CompilerParams(
            collective_id=0, has_side_effects=True, vmem_limit_bytes=63 * 1024 * 1024
        ),
    )(
        reach_attrs.T, w_first, b_first, w_second, b_second, w_out, section_factor,
        bed_slope, seg_count, section_class, down_local, send_list, recv_list,
        area_start, lateral, cotangent,
    )
    vector = jax.ShapeDtypeStruct((hid,), f32)
    large, outflow, grad_lateral, g_first, g_b_first, g_b_second, g_out = pl.pallas_call(
        functools.partial(finish, feat),
        out_shape=(
            jax.ShapeDtypeStruct((n_event, owners, span - 1, 8, 128), f32),
            jax.ShapeDtypeStruct((events, reaches), f32),
            jax.ShapeDtypeStruct((STEPS, events, reaches), f32),
            jax.ShapeDtypeStruct((feat, hid), f32),
            vector,
            vector,
            vector,
        ),
        in_specs=[vmem] * 3,
        out_specs=(hbm, hbm, hbm, vmem, vmem, vmem, vmem),
        scratch_shapes=[dma((3,))],
    )(full, outflow, grad_lateral)
    g_second = large.reshape(hid // 8, hid // 128, 8, 128).transpose(0, 2, 1, 3).reshape(hid, hid)
    return outflow, grad_lateral, g_first, g_b_first, g_second, g_b_second, g_out


def solution(mesh):
    return jax.shard_map(
        functools.partial(body, mesh.shape["basin"], mesh.shape["event"]),
        mesh=mesh,
        in_specs=(
            P("basin", None),
            P(),
            P(),
            P(),
            P(),
            P(),
            P(),
            P("basin"),
            P("basin"),
            P("basin"),
            P("basin"),
            P("basin", None, None),
            P("basin", None, None),
            P("event", "basin"),
            P(None, "event", "basin"),
            P("event", "basin"),
        ),
        out_specs=(P("event", "basin"), P(None, "event", "basin"), P(), P(), P(), P(), P()),
        check_vma=False,
    )
```

time: 98.7 us -> 81.4 us (0.82)
  local copies, waits for them, and re-layouts: 14.4 us -> 0 us
  other arithmetic: 2.37 us -> 0 us
    unnamed x35 -> x0, local copies, waits for them, and re-layouts: 8.44 us -> none
    slice x2 -> x0, local copies, waits for them, and re-layouts: 4.59 us -> none  [the longest x1 3.29 us: body(): full[:, :hid]]
    pallas_call x1, Pallas kernels: 79.4 us -> 75.1 us  [body(): pl.pallas_call(functools.partial(kernel, n, n_event, owners, chunk, scale...]
    pallas_call x0 -> x1, Pallas kernels: none -> 4.25 us  [body(): pl.pallas_call(functools.partial(finish, feat), out_shape=(jax.ShapeDtype...]
    transpose x1 -> x0, local copies, waits for them, and re-layouts: 1.02 us -> none  [body(): small = full[:, hid:hid + feat + 3].T]
where the time goes in v1:
time: 81.4 us; the launch traced here: 79.9 us
  Pallas kernels  79.3 us (97%)
    pallas_call x1, Pallas kernels, body(): pl.pallas_call(functools.partial(kernel, n, n_event, owners, chunk, scale...  75.1 us
    pallas_call x1, Pallas kernels, body(): pl.pallas_call(functools.partial(finish, feat), out_shape=(jax.ShapeDtype...  4.25 us

profile of v1, /device:TPU:9, one launch (start us, length us, event | category | flops | bytes accessed | tf_op | source)
XLA Modules:
  0.0 79.9 jit_solution(18088263027792518868)
XLA Ops:
  0.6 75.1 %shard_map.207 = (f32[32,1536]{1,0:T(8,128)}, f32[3,32,1536]{2,1,0:T(8,128)}, f32[4,8,19,8,128]{4,3,2,1,0:T(8,128)}) custom-call(bf16[32,1536]{1,0:T(8,128)(2,1)} %bitcast.6, bf16[32,768]{1,0:T(8,128)(2,1)} %w_first_h.1, f32[768]{0:T(1024)} %b_first_h.1, bf16[768,768]{1,0:T(8,128)(2,1)} %w_second_h.1, f32[768]{0:T(1024)} %b_second_h.1, ...), custom_call_target="tpu_custom_call" | custom-call | tf_op jit(solution)/shard_map/pallas_call | solution.py:619
  75.7 4.2 %shard_map.208 = (f32[4,8,18,8,128]{4,3,2,1,0:T(8,128)}, f32[32,1536]{1,0:T(8,128)}, f32[3,32,1536]{2,1,0:T(8,128)}, f32[32,768]{1,0:T(8,128)}, f32[768]{0:T(1024)}, /*index=5*/f32[768]{0:T(1024)}, f32[768]{0:T(1024)}) custom-call(f32[4,8,19,8,128]{4,3,2,1,0:T(8,128)} %get-tuple-element.17.full, f32[32,1536]{1,0:T(8,128)} %get-tuple-element.18.flow_in, ...), custom_call_target="tpu_custom_call" | custom-call | tf_op jit(solution)/shard_map/pallas_call | solution.py:668

commit v2 on v1

--- a/solution.py
+++ b/solution.py
@@ -9,6 +9,7 @@
 from jax.sharding import PartitionSpec as P
 
 STEPS = 3
+HALO = 2 * STEPS
 LINKS = 4
 GROUP = 32
 PLACES = 48
@@ -27,7 +28,8 @@
     attrs_h, w_first_h, b_first_h, w_second_h, b_second_h, w_out_h, section_factor,
     bed_slope_h, seg_count_h, section_class_h, down_local_h, send_list_h, recv_list_h,
     area_start_h, lateral_h, cotangent_h,
-    outflow, grad_lateral, full,
+    outflow_h, grad_lateral_h, full_h,
+    outflow, grad_lateral, full, out_sem,
     attrs, w_first, b_first, w_second, b_second, w_out,
     bed_slope, seg_count, section_class, down_local, send_list, recv_list,
     area_start, lateral, cotangent, load_sem,
@@ -37,7 +39,7 @@
     s_send, s_recv,
     x_send, x_recv, r_send, r_recv, px_send, px_recv, pz_send, pz_recv,
     az_send, az_recv, ax_send, ax_recv, ay_send, ay_recv,
-    fa_send, fa_recv, fb_send, fb_recv, tw_send, tw_recv,
+    fa_send, fa_recv, fb_send, fb_recv, tw_send, tw_recv, write_sem,
 ):
     f32, bf16 = jnp.float32, jnp.bfloat16
     me = lax.axis_index("basin")
@@ -83,65 +85,13 @@
             barrier, inc=1, device_id={"event": lax.rem(ev + i, n_event)}, device_id_type=MESH
         )
 
-    for name in ("w_first", "attrs", "b_first", "b_second", "w_out", "w_second"):
+    for name in ("send_list", "attrs", "area_start", "bed_slope", "section_class"):
         loads[name].wait()
 
     extra = attrs.shape[0] - feat
     attrs[feat:, :] = jnp.where(
         lax.broadcasted_iota(jnp.int32, (extra, reaches), 0) == 0, 1.0, 0.0
     ).astype(bf16)
-    w_firstT[...] = jnp.transpose(w_first[...])
-    w_secondT[...] = jnp.transpose(w_second[...])
-    w_out_row = w_out[...].astype(f32).reshape(1, hid)
-    cols[...] = jnp.transpose(jnp.concatenate(
-        [b_first[...].reshape(1, hid), b_second[...].reshape(1, hid), w_out_row,
-         jnp.zeros((5, hid), f32)], axis=0
-    ))
-    w_out_rows = jnp.broadcast_to(w_out_row, (16, hid)).astype(bf16)
-
-    def network(block):
-        where = pl.ds(pl.multiple_of(block * width, 128), width)
-        one = jnp.tanh(
-            jnp.dot(w_firstT[...], attrs[0:feat, where], preferred_element_type=f32) + cols[:, 0:1]
-        )
-        t_one[:, where] = one
-        hidden = one.astype(bf16)
-        h_one[:, where] = hidden
-        two = jnp.tanh(
-            jnp.dot(w_secondT[...], hidden, preferred_element_type=f32) + cols[:, 1:2]
-        )
-        rounded = two.astype(bf16)
-        h_two[:, where] = rounded
-        factor = (cols[:, 2:3] * (1.0 - two * two)).astype(bf16)
-        d_two[:, where] = factor
-        first = t_one[mine, where]
-        lower[:, where] = (
-            jnp.dot(w_second[mine, :], factor, preferred_element_type=f32) * (1.0 - first * first)
-        )
-        return rounded
-
-    logit = jnp.dot(w_out_rows, network(ev), preferred_element_type=f32)[0:1]
-    squash_all[ev] = 1.0 / (1.0 + jnp.exp(-logit))
-
-    pl.semaphore_wait(barrier, n - 1 + n_event - 1)
-
-    def squash_copy(i):
-        return pltpu.make_async_remote_copy(
-            src_ref=squash_all.at[ev],
-            dst_ref=squash_all.at[ev],
-            send_sem=s_send.at[i],
-            recv_sem=s_recv.at[i],
-            device_id={"event": lax.rem(ev + 1 + i, n_event)},
-            device_id_type=MESH,
-        )
-
-    for i in range(n_event - 1):
-        squash_copy(i).start()
-
-    for name in ("send_list", "recv_list", "bed_slope", "section_class", "seg_count", "down_local",
-                 "area_start"):
-        loads[name].wait()
-
     slot_row = lax.broadcasted_iota(jnp.int32, (LINKS * GROUP, 1), 0)
     slot = slot_row % GROUP
     cap = send_list.shape[2]
@@ -163,26 +113,14 @@
         column = jnp.where(slot < cap, column, float(reaches))
         return (jnp.abs(lane_reach - column) < 0.5).astype(bf16)
 
+
     take_send[...] = one_hot_of(send_list, 1)
-    take_recv[...] = one_hot_of(recv_list, -1)
 
     kind = section_class[...].reshape(1, reaches)
     conveyance = jnp.zeros((1, reaches), f32)
     for c in range(section_factor.shape[0]):
         conveyance = jnp.where(kind == c, section_factor[c], conveyance)
     k_base = jnp.sqrt(bed_slope[...].reshape(1, reaches)) * conveyance
-    beta = 1.0 / seg_count[...].reshape(1, reaches).astype(f32)
-    down = down_local[...].reshape(1, reaches)
-    hop = jnp.where(down < reaches, down - lax.broadcasted_iota(jnp.int32, (1, reaches), 1), 0)
-    masks = [(hop == d).astype(f32) for d in range(1, 9)]
-
-    network(lax.rem(ev + 1, n_event))
-
-    for i in range(n_event - 1):
-        squash_copy(i).wait_recv()
-    squash = jnp.concatenate([squash_all[e] for e in range(n_event)], axis=1)
-    rough = 0.02 + 0.08 * squash
-    rate = k_base / rough
     lane_group = lax.broadcasted_iota(jnp.int32, (8, 128), 1) // GROUP
     blocks = events // 8
 
@@ -196,9 +134,11 @@
             device_id_type=MESH,
         )
 
-    def send(index, field, matrix, sign):
+    def pick(field, matrix):
         both = lax.dot_general(split_two(field), matrix[...], NT, preferred_element_type=f32)
-        picked = both[:events] + both[events:]
+        return both[:events] + both[events:]
+
+    def send(index, picked, sign):
         for k in range(LINKS):
             packed = jnp.zeros((8, 128), f32)
             for q in range(blocks):
@@ -210,7 +150,7 @@
             out_msg[index, k] = packed
             message(index, k, sign).start()
 
-    def receive(index, matrix, sign):
+    def receive(index, sign):
         for k in range(LINKS):
             message(index, k, sign).wait_recv()
         pieces = []
@@ -223,35 +163,122 @@
                     piece = pltpu.roll(piece, shift, 1)
                 got = jnp.where(lane_group == k, piece, got)
             pieces.append(got)
-        both = jnp.dot(
-            split_two(jnp.concatenate(pieces, axis=0)), matrix[...], preferred_element_type=f32
-        )
+        return jnp.concatenate(pieces, axis=0)
+
+    def scatter(got, matrix):
+        both = jnp.dot(split_two(got), matrix[...], preferred_element_type=f32)
         return both[:events] + both[events:]
 
     def power(area):
         return jnp.exp((2.0 / 3.0) * jnp.log(area))
 
+
     areas = [area_start[...]]
     powers = [power(areas[0])]
+    plain = areas[0] * powers[0]
+    outer = pick(k_base * plain, take_send)
+    inputs = lax.dot_general(attrs[0:feat, :], take_send[...], NT, preferred_element_type=f32)
+
+    pl.semaphore_wait(barrier, n - 1 + n_event - 1)
+    send(HALO, inputs, 1)
+    send(0, outer, 1)
+
+    for name in ("w_first", "b_first", "b_second", "w_out", "w_second"):
+        loads[name].wait()
+
+    w_firstT[...] = jnp.transpose(w_first[...])
+    w_secondT[...] = jnp.transpose(w_second[...])
+    w_out_row = w_out[...].astype(f32).reshape(1, hid)
+    cols[...] = jnp.transpose(jnp.concatenate(
+        [b_first[...].reshape(1, hid), b_second[...].reshape(1, hid), w_out_row,
+         jnp.zeros((5, hid), f32)], axis=0
+    ))
+    w_out_rows = jnp.broadcast_to(w_out_row, (16, hid)).astype(bf16)
+
+    def network(block):
+        where = pl.ds(pl.multiple_of(block * width, 128), width)
+        one = jnp.tanh(
+            jnp.dot(w_firstT[...], attrs[0:feat, where], preferred_element_type=f32) + cols[:, 0:1]
+        )
+        t_one[:, where] = one
+        hidden = one.astype(bf16)
+        h_one[:, where] = hidden
+        two = jnp.tanh(
+            jnp.dot(w_secondT[...], hidden, preferred_element_type=f32) + cols[:, 1:2]
+        )
+        rounded = two.astype(bf16)
+        h_two[:, where] = rounded
+        factor = (cols[:, 2:3] * (1.0 - two * two)).astype(bf16)
+        d_two[:, where] = factor
+        first = t_one[mine, where]
+        lower[:, where] = (
+            jnp.dot(w_second[mine, :], factor, preferred_element_type=f32) * (1.0 - first * first)
+        )
+        return rounded
+
+    logit = jnp.dot(w_out_rows, network(ev), preferred_element_type=f32)[0:1]
+    squash_all[ev] = 1.0 / (1.0 + jnp.exp(-logit))
+
+    def squash_copy(i):
+        return pltpu.make_async_remote_copy(
+            src_ref=squash_all.at[ev],
+            dst_ref=squash_all.at[ev],
+            send_sem=s_send.at[i],
+            recv_sem=s_recv.at[i],
+            device_id={"event": lax.rem(ev + 1 + i, n_event)},
+            device_id_type=MESH,
+        )
+
+    for i in range(n_event - 1):
+        squash_copy(i).start()
+
+    for name in ("recv_list", "seg_count", "down_local", "lateral"):
+        loads[name].wait()
+    take_recv[...] = one_hot_of(recv_list, -1)
+    beta = 1.0 / seg_count[...].reshape(1, reaches).astype(f32)
+    down = down_local[...].reshape(1, reaches)
+    hop = jnp.where(down < reaches, down - lax.broadcasted_iota(jnp.int32, (1, reaches), 1), 0)
+    masks = [(hop == d).astype(f32) for d in range(1, 9)]
+
+
+    def hidden_of(weight, x, column):
+        return jnp.tanh(
+            jnp.dot(weight[...], x, preferred_element_type=f32) + cols[:, column : column + 1]
+        ).astype(bf16)
+
+    around = receive(HALO, 1).astype(bf16)
+    around = hidden_of(w_secondT, hidden_of(w_firstT, around, 0), 1)
+    around = jnp.dot(w_out_rows, around, preferred_element_type=f32)[0:1]
+    flow_in = receive(0, 1) / (0.02 + 0.08 * (1.0 / (1.0 + jnp.exp(-around))))
+    flow_in = scatter(flow_in, take_recv)
+
+    for i in range(n_event - 1):
+        squash_copy(i).wait_recv()
+    squash = jnp.concatenate([squash_all[e] for e in range(n_event)], axis=1)
+    rough = 0.02 + 0.08 * squash
+    rate = k_base / rough
     shrinks = []
     for t in range(STEPS):
         area, p = areas[t], powers[t]
         flow = rate * area * p
-        send(t, flow, take_send, 1)
-        if t == 0:
-            loads["lateral"].wait()
+        if t > 0:
+            send(t, pick(flow, take_send), 1)
         inflow = lateral[t]
         for d in range(1, 9):
             inflow = inflow + pltpu.roll(flow * masks[d - 1], d, 1)
         shrink = 1.0 / (1.0 + beta * rate * p)
         shrinks.append(shrink)
-        if t < n_event - 2:
-            network(lax.rem(ev + 2 + t, n_event))
-        inflow = inflow + receive(t, take_recv, 1)
+        if t > 0:
+            if t < n_event:
+                network(lax.rem(ev + t, n_event))
+            flow_in = scatter(receive(t, 1), take_recv)
+        inflow = inflow + flow_in
         areas.append((area + beta * inflow) * shrink)
         powers.append(power(areas[t + 1]))
     emitted = areas[STEPS] * powers[STEPS]
     outflow[...] = rate * emitted
+    write_flow = pltpu.make_async_copy(outflow, outflow_h, out_sem.at[0])
+    write_flow.start()
     loads["cotangent"].wait()
     g_area = cotangent[...] * rate * (5.0 / 3.0) * powers[STEPS]
     g_rate = cotangent[...] * emitted
@@ -260,16 +287,21 @@
         inner = g_area * shrinks[t]
         g_inflow = inner * beta
         grad_lateral[t] = g_inflow
-        send(index, g_inflow, take_recv, -1)
+        send(index, pick(g_inflow, take_recv), -1)
         g_flow = jnp.zeros((events, reaches), f32)
         for d in range(1, 9):
             g_flow = g_flow + masks[d - 1] * pltpu.roll(g_inflow, reaches - d, 1)
         drop = g_inflow * areas[t + 1] * powers[t]
         g_rate = g_rate - drop
         g_area = inner - (2.0 / 3.0) * rate * drop / areas[t]
-        g_flow = g_flow + receive(index, take_send, -1)
+        if t == STEPS - 1:
+            for block in range(STEPS, n_event):
+                network(lax.rem(ev + block, n_event))
+        g_flow = g_flow + scatter(receive(index, -1), take_send)
         g_rate = g_rate + g_flow * areas[t] * powers[t]
         g_area = g_area + (5.0 / 3.0) * rate * powers[t] * g_flow
+    write_lateral = pltpu.make_async_copy(grad_lateral, grad_lateral_h, out_sem.at[1])
+    write_lateral.start()
     rate_out[...] = jnp.sum(g_rate, axis=0, keepdims=True)
 
     def rate_copy(i):
@@ -393,6 +425,16 @@
 
     each(0, line, start_pair)
 
+    for i in range(n_event - 1):
+        squash_copy(i).wait_send()
+    for index in range(HALO + 1):
+        for k in range(LINKS):
+            message(index, k, 1).wait_send()
+    for i in range(n_event - 1):
+        rate_copy(i).wait_send()
+    write_flow.wait()
+    write_lateral.wait()
+
     def add_pair(j):
         z = far(j)
 
@@ -504,14 +546,6 @@
         pl.loop(0, line)(second_hop)
         pl.loop(0, line)(corner)
 
-    for i in range(n_event - 1):
-        squash_copy(i).wait_send()
-    for index in range(2 * STEPS):
-        for k in range(LINKS):
-            message(index, k, 1).wait_send()
-    for i in range(n_event - 1):
-        rate_copy(i).wait_send()
-
     def drain(z):
         when_owner(device(z, 1 - low), lambda: pair_sum(z, 1 - low).wait_send())
 
@@ -532,29 +566,43 @@
 
     each(0, line, drain)
 
+    def write_full(z):
+        where = pl.ds(2 * z, 2)
+        return pltpu.make_async_copy(full.at[:, where], full_h.at[:, where], write_sem.at[z])
+
     def arrive(j):
         z = near(j)
 
         def go():
             to_twin(0, twin, z).wait_recv()
             to_twin(1, twin_half, z).wait_recv()
+            write_full(z).start()
 
         when_owner(2 * z, go)
 
     each(0, line, arrive)
+    each(0, line, lambda j: when_owner(2 * near(j), lambda: write_full(near(j)).wait()))
 
 
 def finish(
-    feat, full, flow_in, lateral_in,
-    large, flow_out, lateral_out, w_first, b_first, b_second, w_out, sems,
+    feat, full_in, flow_in, lateral_in,
+    large, flow_out, lateral_out, w_first, b_first, b_second, w_out,
+    full, flow, lateral, sems,
 ):
     last = full.shape[2] - 1
-    copies = [
-        pltpu.make_async_copy(full.at[:, :, pl.ds(0, last)], large, sems.at[0]),
-        pltpu.make_async_copy(lateral_in, lateral_out, sems.at[1]),
-        pltpu.make_async_copy(flow_in, flow_out, sems.at[2]),
-    ]
-    for copy in copies:
+    middle = full.shape[0] // 2
+    steps = []
+    for side in range(2):
+        where = pl.ds(side * middle, middle)
+        steps.append((full_in.at[where], full.at[where], full.at[where, :, pl.ds(0, last)], large.at[where]))
+    steps.append((lateral_in, lateral, lateral, lateral_out))
+    steps.append((flow_in, flow, flow, flow_out))
+    reads = [pltpu.make_async_copy(x[0], x[1], sems.at[0, i]) for i, x in enumerate(steps)]
+    copies = [pltpu.make_async_copy(x[2], x[3], sems.at[1, i]) for i, x in enumerate(steps)]
+    for read in reads:
+        read.start()
+    for read, copy in zip(reads, copies):
+        read.wait()
         copy.start()
     n_event = full.shape[0]
     first_half = lax.broadcasted_iota(jnp.int32, (8, 128), 1) < 64
@@ -624,8 +672,12 @@
             jax.ShapeDtypeStruct((n_event, owners, span, 8, 128), f32),
         ),
         in_specs=[hbm] * 6 + [smem] + [hbm] * 9,
-        out_specs=(vmem,) * 3,
+        out_specs=(hbm,) * 3,
         scratch_shapes=[
+            pltpu.VMEM((events, reaches), f32),
+            pltpu.VMEM((STEPS, events, reaches), f32),
+            pltpu.VMEM((n_event, owners, span, 8, 128), f32),
+            dma((2,)),
             pltpu.VMEM((PLACES, reaches), bf16),
             held(w_first), held(b_first), held(w_second), held(b_second), held(w_out),
             held(bed_slope), held(seg_count), held(section_class), held(down_local),
@@ -642,19 +694,19 @@
             pltpu.VMEM((n_event, 1, reaches // n_event), f32),
             pltpu.VMEM((LINKS * GROUP, reaches), bf16),
             pltpu.VMEM((LINKS * GROUP, reaches), bf16),
-            pltpu.VMEM((2 * STEPS, LINKS, 8, 128), f32),
-            pltpu.VMEM((2 * STEPS, LINKS, 8, 128), f32),
+            pltpu.VMEM((HALO + 1, LINKS, 8, 128), f32),
+            pltpu.VMEM((HALO + 1, LINKS, 8, 128), f32),
             pltpu.VMEM((1, reaches), f32),
             pltpu.VMEM((n_event - 1, 1, reaches), f32),
             pltpu.VMEM((owners, span, 8, 128), f32),
             pltpu.VMEM((line, span, 8, 128), f32),
             pltpu.VMEM((line, span, 8, 128), f32),
             dma((n_event - 1,)), dma((n_event - 1,)),
-            dma((2 * STEPS, LINKS)), dma((2 * STEPS, LINKS)),
+            dma((HALO + 1, LINKS)), dma((HALO + 1, LINKS)),
             dma((n_event - 1,)), dma((n_event - 1,)),
             dma((line,)), dma((line,)), dma((line,)), dma((line,)),
             dma((line,)), dma((line,)), dma((line,)), dma((line,)), dma((line,)), dma((line,)),
-            dma((line,)), dma((line,)), dma((line,)), dma((line,)), dma((2, line)), dma((2, line)),
+            dma((line,)), dma((line,)), dma((line,)), dma((line,)), dma((2, line)), dma((2, line)), dma((line,)),
         ],
         compiler_params=pltpu.CompilerParams(
             collective_id=0, has_side_effects=True, vmem_limit_bytes=63 * 1024 * 1024
@@ -676,9 +728,9 @@
             vector,
             vector,
         ),
-        in_specs=[vmem] * 3,
+        in_specs=[hbm] * 3,
         out_specs=(hbm, hbm, hbm, vmem, vmem, vmem, vmem),
-        scratch_shapes=[dma((3,))],
+        scratch_shapes=[held(full), held(outflow), held(grad_lateral), dma((2, 4))],
     )(full, outflow, grad_lateral)
     g_second = large.reshape(hid // 8, hid // 128, 8, 128).transpose(0, 2, 1, 3).reshape(hid, hid)
     return outflow, grad_lateral, g_first, g_b_first, g_second, g_b_second, g_out

time: 81.4 us -> 77.8 us (0.956)
  Pallas kernels: 79.3 us -> 76 us
    pallas_call x1, Pallas kernels: 75.1 us -> 72.3 us  [body(): pl.pallas_call(functools.partial(kernel, n, n_event, owners, chunk, scale...]
where the time goes in v2:
time: 77.8 us; the launch traced here: 76.6 us
  Pallas kernels  76 us (98%)
    pallas_call x1, Pallas kernels, body(): pl.pallas_call(functools.partial(kernel, n, n_event, owners, chunk, scale...  72.3 us
    pallas_call x1, Pallas kernels, body(): pl.pallas_call(functools.partial(finish, feat), out_shape=(jax.ShapeDtype...  3.66 us

profile of v2, /device:TPU:9, one launch (start us, length us, event | category | flops | bytes accessed | tf_op | source)
XLA Modules:
  0.0 76.6 jit_solution(7238355132211499436)
XLA Ops:
  0.6 72.3 %shard_map.207 = (f32[32,1536]{1,0:T(8,128)}, f32[3,32,1536]{2,1,0:T(8,128)}, f32[4,8,19,8,128]{4,3,2,1,0:T(8,128)}) custom-call(bf16[32,1536]{1,0:T(8,128)(2,1)} %bitcast.6, bf16[32,768]{1,0:T(8,128)(2,1)} %w_first_h.1, f32[768]{0:T(1024)} %b_first_h.1, bf16[768,768]{1,0:T(8,128)(2,1)} %w_second_h.1, f32[768]{0:T(1024)} %b_second_h.1, ...), custom_call_target="tpu_custom_call" | custom-call | tf_op jit(solution)/shard_map/pallas_call | solution.py:667
  73.0 3.7 %shard_map.208 = (f32[4,8,18,8,128]{4,3,2,1,0:T(8,128)}, f32[32,1536]{1,0:T(8,128)}, f32[3,32,1536]{2,1,0:T(8,128)}, f32[32,768]{1,0:T(8,128)}, f32[768]{0:T(1024)}, /*index=5*/f32[768]{0:T(1024)}, f32[768]{0:T(1024)}) custom-call(f32[4,8,19,8,128]{4,3,2,1,0:T(8,128)} %get-tuple-element.17.full_in, f32[32,1536]{1,0:T(8,128)} %get-tuple-element.18.flow_in, ...), custom_call_target="tpu_custom_call" | custom-call | tf_op jit(solution)/shard_map/pallas_call | solution.py:720

commit v3 on v2

--- a/solution.py
+++ b/solution.py
@@ -381,6 +381,7 @@
     twin_half = lax.rem(twin + n_event // 2, n_event)
     span = slab.shape[1]
     cut = (span + 1) // 2
+    halves = (pl.ds(0, cut), pl.ds(cut, span - cut))
 
     def each(first, last, work):
         if last - first <= 4:
@@ -402,28 +403,29 @@
     def device(z, parity):
         return 2 * z + parity
 
-    def pair_sum(z, parity):
+    def pair_sum(h, z, parity):
         return pltpu.make_async_remote_copy(
-            src_ref=slab.at[device(z, parity)], dst_ref=rs_pair.at[z],
-            send_sem=px_send.at[z], recv_sem=px_recv.at[z],
+            src_ref=slab.at[device(z, parity), halves[h]], dst_ref=rs_pair.at[z, halves[h]],
+            send_sem=px_send.at[h, z], recv_sem=px_recv.at[h, z],
             device_id={"basin": pair}, device_id_type=MESH,
         )
 
-    def line_sum(z, sender):
+    def line_sum(h, z, sender):
         return pltpu.make_async_remote_copy(
-            src_ref=rs_pair.at[z], dst_ref=rs_line.at[sender],
-            send_sem=pz_send.at[z], recv_sem=pz_recv.at[sender],
+            src_ref=rs_pair.at[z, halves[h]], dst_ref=rs_line.at[sender, halves[h]],
+            send_sem=pz_send.at[h, z], recv_sem=pz_recv.at[h, sender],
             device_id={"basin": device(z, low)}, device_id_type=MESH,
         )
 
     def far(j):
         return near(line - 1 - j)
 
-    def start_pair(j):
+    def start_pair(h, j):
         z = far(j)
-        when_owner(device(z, 1 - low), lambda: pair_sum(z, 1 - low).start())
-
-    each(0, line, start_pair)
+        when_owner(device(z, 1 - low), lambda: pair_sum(h, z, 1 - low).start())
+
+    for h in range(2):
+        each(0, line, functools.partial(start_pair, h))
 
     for i in range(n_event - 1):
         squash_copy(i).wait_send()
@@ -435,50 +437,44 @@
     write_flow.wait()
     write_lateral.wait()
 
-    def add_pair(j):
+    def add_pair(h, j):
         z = far(j)
 
         def go():
-            pair_sum(z, 1 - low).wait_recv()
-            rs_pair[z] = rs_pair[z] + slab[device(z, low)]
+            pair_sum(h, z, 1 - low).wait_recv()
+            rs_pair[z, halves[h]] = rs_pair[z, halves[h]] + slab[device(z, low), halves[h]]
 
             @pl.when(z != spot)
             def _():
-                line_sum(z, spot).start()
+                line_sum(h, z, spot).start()
 
         when_owner(device(z, low), go)
 
-    each(0, line, add_pair)
-
-    whole = pl.ds(0, span)
-    upper = pl.ds(0, cut)
-    under = pl.ds(cut, span - cut)
-
-    def move(event, at, rows, sems, slot, target):
-        ref = full.at[event, at, rows]
+    def move(event, at, h, sems, slot, target):
+        ref = full.at[event, at, halves[h]]
         return pltpu.make_async_remote_copy(
             src_ref=ref, dst_ref=ref, send_sem=sems[0].at[slot], recv_sem=sems[1].at[slot],
             device_id=target, device_id_type=MESH,
         )
 
-    def to_line(source, peer):
-        ref = full.at[ev, device(source, low)]
+    def to_line(h, source, peer):
+        ref = full.at[ev, device(source, low), halves[h]]
         return pltpu.make_async_remote_copy(
-            src_ref=ref, dst_ref=ref, send_sem=az_send.at[peer], recv_sem=az_recv.at[source],
+            src_ref=ref, dst_ref=ref, send_sem=az_send.at[h, peer], recv_sem=az_recv.at[h, source],
             device_id={"basin": device(peer, low)}, device_id_type=MESH,
         )
 
-    def to_pair(z, parity):
-        return move(ev, device(z, parity), whole, (ax_send, ax_recv), z, {"basin": pair})
-
-    def to_half(event, z):
-        return move(event, device(z, low), whole, (ay_send, ay_recv), z, {"event": half})
+    def to_pair(h, z, parity):
+        return move(ev, device(z, parity), h, (ax_send.at[h], ax_recv.at[h]), z, {"basin": pair})
+
+    def to_half(h, event, z):
+        return move(event, device(z, low), h, (ay_send.at[h], ay_recv.at[h]), z, {"event": half})
 
     def on_half(event, z):
-        return move(event, device(z, 1 - low), upper, (fa_send, fa_recv), z, {"event": half})
+        return move(event, device(z, 1 - low), 0, (fa_send, fa_recv), z, {"event": half})
 
     def on_pair(z, parity):
-        return move(half, device(z, parity), under, (fb_send, fb_recv), z, {"basin": pair})
+        return move(half, device(z, parity), 1, (fb_send, fb_recv), z, {"basin": pair})
 
     def to_twin(side, event, z):
         ref = full.at[event, pl.ds(2 * z, 2)]
@@ -487,38 +483,49 @@
             device_id={"event": twin}, device_id_type=MESH,
         )
 
-    def own():
-        def add(i, total):
-            sender = lax.rem(spot + line - i, line)
-            line_sum(spot, sender).wait_recv()
-            return total + rs_line[sender]
-
-        full[ev, me] = lax.fori_loop(1, line, add, rs_pair[spot])
-        each(1, line, lambda j: to_line(spot, near(j)).start())
-        to_pair(spot, low).start()
-        to_half(ev, spot).start()
-
-    when_owner(me, own)
-
-    def from_line(j):
+    def own(h):
+        def go():
+            total = rs_pair[spot, halves[h]]
+            if line <= 4:
+                for j in range(1, line):
+                    sender = near(j)
+                    line_sum(h, spot, sender).wait_recv()
+                    total = total + rs_line[sender, halves[h]]
+            else:
+
+                def add(i, total):
+                    sender = lax.rem(spot + line - i, line)
+                    line_sum(h, spot, sender).wait_recv()
+                    return total + rs_line[sender, halves[h]]
+
+                total = lax.fori_loop(1, line, add, total)
+            full[ev, me, halves[h]] = total
+            each(1, line, lambda j: to_line(h, spot, near(j)).start())
+            to_pair(h, spot, low).start()
+            to_half(h, ev, spot).start()
+
+        when_owner(me, go)
+
+    def from_line(h, j):
         z = near(j)
 
         def go():
-            to_line(z, spot).wait_recv()
-            to_pair(z, low).start()
-            to_half(ev, z).start()
+            to_line(h, z, spot).wait_recv()
+            to_pair(h, z, low).start()
+            to_half(h, ev, z).start()
 
         when_owner(device(z, low), go)
 
-    def second_hop(j):
+    def hop(h, j):
         z = near(j)
 
         def go():
-            to_pair(z, 1 - low).wait_recv()
-            on_half(ev, z).start()
-            to_twin(0, ev, z).start()
-            to_half(half, z).wait_recv()
-            on_pair(z, low).start()
+            if h == 0:
+                to_pair(0, z, 1 - low).wait_recv()
+                on_half(ev, z).start()
+            else:
+                to_half(1, half, z).wait_recv()
+                on_pair(z, low).start()
 
         when_owner(2 * z, go)
 
@@ -526,37 +533,56 @@
         z = near(j)
 
         def go():
+            to_pair(1, z, 1 - low).wait_recv()
+            to_twin(0, ev, z).start()
+            to_half(0, half, z).wait_recv()
             on_half(half, z).wait_recv()
             on_pair(z, 1 - low).wait_recv()
             to_twin(1, half, z).start()
 
         when_owner(2 * z, go)
 
-    if line <= 4:
-        for j in range(1, line):
-            from_line(j)
-            second_hop(j - 1)
-            if j >= 2:
-                corner(j - 2)
-        second_hop(line - 1)
-        corner(line - 2)
-        corner(line - 1)
+    if line == 4:
+        for j in range(line):
+            add_pair(0, j)
+        add_pair(1, 0)
+        add_pair(1, 1)
+        own(0)
+        add_pair(1, 2)
+        add_pair(1, 3)
+        hop(0, 0)
+        from_line(0, 1)
+        own(1)
+        for work, h, j in (
+            (from_line, 0, 2), (from_line, 0, 3), (hop, 0, 1), (hop, 1, 0), (from_line, 1, 1),
+            (hop, 0, 2), (from_line, 1, 2), (hop, 0, 3), (from_line, 1, 3), (hop, 1, 1),
+            (hop, 1, 2), (hop, 1, 3),
+        ):
+            work(h, j)
     else:
-        pl.loop(1, line)(from_line)
-        pl.loop(0, line)(second_hop)
-        pl.loop(0, line)(corner)
+        for h in range(2):
+            each(0, line, functools.partial(add_pair, h))
+        for h in range(2):
+            own(h)
+        for h in range(2):
+            each(1, line, functools.partial(from_line, h))
+        for h in range(2):
+            each(0, line, functools.partial(hop, h))
+    each(0, line, corner)
 
     def drain(z):
-        when_owner(device(z, 1 - low), lambda: pair_sum(z, 1 - low).wait_send())
-
-        @pl.when(z != spot)
-        def _():
-            when_owner(device(z, low), lambda: line_sum(z, spot).wait_send())
-            when_owner(me, lambda: to_line(spot, z).wait_send())
+        for h in range(2):
+            when_owner(device(z, 1 - low), lambda: pair_sum(h, z, 1 - low).wait_send())
+
+            @pl.when(z != spot)
+            def _():
+                when_owner(device(z, low), lambda: line_sum(h, z, spot).wait_send())
+                when_owner(me, lambda: to_line(h, spot, z).wait_send())
 
         def go():
-            to_pair(z, low).wait_send()
-            to_half(ev, z).wait_send()
+            for h in range(2):
+                to_pair(h, z, low).wait_send()
+                to_half(h, ev, z).wait_send()
             on_half(ev, z).wait_send()
             on_pair(z, low).wait_send()
             to_twin(0, ev, z).wait_send()
@@ -704,9 +730,11 @@
             dma((n_event - 1,)), dma((n_event - 1,)),
             dma((HALO + 1, LINKS)), dma((HALO + 1, LINKS)),
             dma((n_event - 1,)), dma((n_event - 1,)),
-            dma((line,)), dma((line,)), dma((line,)), dma((line,)),
-            dma((line,)), dma((line,)), dma((line,)), dma((line,)), dma((line,)), dma((line,)),
-            dma((line,)), dma((line,)), dma((line,)), dma((line,)), dma((2, line)), dma((2, line)), dma((line,)),
+            dma((2, line)), dma((2, line)), dma((2, line)), dma((2, line)),
+            dma((2, line)), dma((2, line)), dma((2, line)), dma((2, line)),
+            dma((2, line)), dma((2, line)),
+            dma((line,)), dma((line,)), dma((line,)), dma((line,)), dma((2, line)), dma((2, line)),
+            dma((line,)),
         ],
         compiler_params=pltpu.CompilerParams(
             collective_id=0, has_side_effects=True, vmem_limit_bytes=63 * 1024 * 1024

time: 77.8 us -> 75 us (0.964)
  Pallas kernels: 76 us -> 73.3 us
    pallas_call x1, Pallas kernels: 72.3 us -> 69.6 us  [body(): pl.pallas_call(functools.partial(kernel, n, n_event, owners, chunk, scale...]
where the time goes in v3:
time: 75 us; the launch traced here: 73.9 us
  Pallas kernels  73.3 us (98%)
    pallas_call x1, Pallas kernels, body(): pl.pallas_call(functools.partial(kernel, n, n_event, owners, chunk, scale...  69.6 us
    pallas_call x1, Pallas kernels, body(): pl.pallas_call(functools.partial(finish, feat), out_shape=(jax.ShapeDtype...  3.66 us

profile of v3, /device:TPU:9, one launch (start us, length us, event | category | flops | bytes accessed | tf_op | source)
XLA Modules:
  0.0 73.9 jit_solution(384816696754963284)
XLA Ops:
  0.6 69.6 %shard_map.207 = (f32[32,1536]{1,0:T(8,128)}, f32[3,32,1536]{2,1,0:T(8,128)}, f32[4,8,19,8,128]{4,3,2,1,0:T(8,128)}) custom-call(bf16[32,1536]{1,0:T(8,128)(2,1)} %bitcast.6, bf16[32,768]{1,0:T(8,128)(2,1)} %w_first_h.1, f32[768]{0:T(1024)} %b_first_h.1, bf16[768,768]{1,0:T(8,128)(2,1)} %w_second_h.1, f32[768]{0:T(1024)} %b_second_h.1, ...), custom_call_target="tpu_custom_call" | custom-call | tf_op jit(solution)/shard_map/pallas_call | solution.py:693
  70.3 3.7 %shard_map.208 = (f32[4,8,18,8,128]{4,3,2,1,0:T(8,128)}, f32[32,1536]{1,0:T(8,128)}, f32[3,32,1536]{2,1,0:T(8,128)}, f32[32,768]{1,0:T(8,128)}, f32[768]{0:T(1024)}, /*index=5*/f32[768]{0:T(1024)}, f32[768]{0:T(1024)}) custom-call(f32[4,8,19,8,128]{4,3,2,1,0:T(8,128)} %get-tuple-element.17.full_in, f32[32,1536]{1,0:T(8,128)} %get-tuple-element.18.flow_in, ...), custom_call_target="tpu_custom_call" | custom-call | tf_op jit(solution)/shard_map/pallas_call | solution.py:748

commit v4 on v3

--- a/solution.py
+++ b/solution.py
@@ -9,12 +9,14 @@
 from jax.sharding import PartitionSpec as P
 
 STEPS = 3
+TINY = 1e-30
 HALO = 2 * STEPS
 LINKS = 4
 GROUP = 32
 PLACES = 48
 MESH = pl.DeviceIdType.MESH
 NT = (((1,), (1,)), ((), ()))
+NN = (((1,), (0,)), ((), ()))
 
 
 def split_two(x):
@@ -34,7 +36,7 @@
     bed_slope, seg_count, section_class, down_local, send_list, recv_list,
     area_start, lateral, cotangent, load_sem,
     w_firstT, w_secondT, cols,
-    t_one, h_one, d_two, h_two, lower, squash_all, take_send, take_recv,
+    t_one, h_one, d_two, h_two, lower, squash_all, take_send, take_recv, overlap,
     out_msg, in_msg, rate_out, rate_in, slab, rs_pair, rs_line,
     s_send, s_recv,
     x_send, x_recv, r_send, r_recv, px_send, px_recv, pz_send, pz_recv,
@@ -53,37 +55,37 @@
     mine = pl.ds(base, part)
     width = reaches // n_event
 
+    barrier = pltpu.get_barrier_semaphore()
+
+    @pl.loop(1, n)
+    def _(i):
+        pl.semaphore_signal(barrier, inc=1, device_id={"basin": lax.rem(me + i, n)}, device_id_type=MESH)
+
+    for i in range(1, n_event):
+        pl.semaphore_signal(
+            barrier, inc=1, device_id={"event": lax.rem(ev + i, n_event)}, device_id_type=MESH
+        )
+
     loads = {}
     for name, source, target in (
+        ("send_list", send_list_h, send_list),
+        ("attrs", attrs_h, attrs.at[pl.ds(0, feat)]),
+        ("area_start", area_start_h, area_start),
+        ("bed_slope", bed_slope_h, bed_slope),
+        ("section_class", section_class_h, section_class),
+        ("w_second", w_second_h, w_second),
         ("w_first", w_first_h, w_first),
-        ("attrs", attrs_h, attrs.at[pl.ds(0, feat)]),
         ("b_first", b_first_h, b_first),
         ("b_second", b_second_h, b_second),
         ("w_out", w_out_h, w_out),
-        ("w_second", w_second_h, w_second),
-        ("send_list", send_list_h, send_list),
         ("recv_list", recv_list_h, recv_list),
-        ("bed_slope", bed_slope_h, bed_slope),
-        ("section_class", section_class_h, section_class),
         ("seg_count", seg_count_h, seg_count),
         ("down_local", down_local_h, down_local),
-        ("area_start", area_start_h, area_start),
         ("lateral", lateral_h, lateral),
         ("cotangent", cotangent_h, cotangent),
     ):
         loads[name] = pltpu.make_async_copy(source, target, load_sem.at[len(loads)])
         loads[name].start()
-
-    barrier = pltpu.get_barrier_semaphore()
-
-    @pl.loop(1, n)
-    def _(i):
-        pl.semaphore_signal(barrier, inc=1, device_id={"basin": lax.rem(me + i, n)}, device_id_type=MESH)
-
-    for i in range(1, n_event):
-        pl.semaphore_signal(
-            barrier, inc=1, device_id={"event": lax.rem(ev + i, n_event)}, device_id_type=MESH
-        )
 
     for name in ("send_list", "attrs", "area_start", "bed_slope", "section_class"):
         loads[name].wait()
@@ -134,9 +136,16 @@
             device_id_type=MESH,
         )
 
-    def pick(field, matrix):
-        both = lax.dot_general(split_two(field), matrix[...], NT, preferred_element_type=f32)
-        return both[:events] + both[events:]
+    def pick(fields, matrix):
+        rows = fields[0].shape[0]
+        both = lax.dot_general(
+            jnp.concatenate([split_two(field) for field in fields], axis=0), matrix[...], NT,
+            preferred_element_type=f32,
+        )
+        return [
+            both[2 * rows * i : 2 * rows * i + rows] + both[2 * rows * i + rows : 2 * rows * (i + 1)]
+            for i in range(len(fields))
+        ]
 
     def send(index, picked, sign):
         for k in range(LINKS):
@@ -167,16 +176,24 @@
 
     def scatter(got, matrix):
         both = jnp.dot(split_two(got), matrix[...], preferred_element_type=f32)
+        rows = got.shape[0]
+        return both[:rows] + both[rows:]
+
+    def cross(got, dims):
+        both = lax.dot_general(split_two(got), overlap[...], dims, preferred_element_type=f32)
         return both[:events] + both[events:]
 
     def power(area):
         return jnp.exp((2.0 / 3.0) * jnp.log(area))
+
+    def slot_power(area):
+        return power(jnp.maximum(area, TINY))
 
 
     areas = [area_start[...]]
     powers = [power(areas[0])]
     plain = areas[0] * powers[0]
-    outer = pick(k_base * plain, take_send)
+    outer, slot_plain = pick([k_base * plain, plain], take_send)
     inputs = lax.dot_general(attrs[0:feat, :], take_send[...], NT, preferred_element_type=f32)
 
     pl.semaphore_wait(barrier, n - 1 + n_event - 1)
@@ -195,8 +212,8 @@
     ))
     w_out_rows = jnp.broadcast_to(w_out_row, (16, hid)).astype(bf16)
 
-    def network(block):
-        where = pl.ds(pl.multiple_of(block * width, 128), width)
+    def network(start, length):
+        where = pl.ds(pl.multiple_of(start * 128, 128), length)
         one = jnp.tanh(
             jnp.dot(w_firstT[...], attrs[0:feat, where], preferred_element_type=f32) + cols[:, 0:1]
         )
@@ -216,7 +233,7 @@
         )
         return rounded
 
-    logit = jnp.dot(w_out_rows, network(ev), preferred_element_type=f32)[0:1]
+    logit = jnp.dot(w_out_rows, network(ev * (width // 128), width), preferred_element_type=f32)[0:1]
     squash_all[ev] = 1.0 / (1.0 + jnp.exp(-logit))
 
     def squash_copy(i):
@@ -235,6 +252,9 @@
     for name in ("recv_list", "seg_count", "down_local", "lateral"):
         loads[name].wait()
     take_recv[...] = one_hot_of(recv_list, -1)
+    overlap[...] = lax.dot_general(
+        take_send[...], take_recv[...], NT, preferred_element_type=f32
+    ).astype(bf16)
     beta = 1.0 / seg_count[...].reshape(1, reaches).astype(f32)
     down = down_local[...].reshape(1, reaches)
     hop = jnp.where(down < reaches, down - lax.broadcasted_iota(jnp.int32, (1, reaches), 1), 0)
@@ -249,37 +269,52 @@
     around = receive(HALO, 1).astype(bf16)
     around = hidden_of(w_secondT, hidden_of(w_firstT, around, 0), 1)
     around = jnp.dot(w_out_rows, around, preferred_element_type=f32)[0:1]
-    flow_in = receive(0, 1) / (0.02 + 0.08 * (1.0 / (1.0 + jnp.exp(-around))))
-    flow_in = scatter(flow_in, take_recv)
+    got = receive(0, 1) / (0.02 + 0.08 * (1.0 / (1.0 + jnp.exp(-around))))
+
+    units = reaches // 128
+    begin = (ev + 1) * (width // 128)
+    odd = lax.rem(begin, 2)
+    pieces_left = [(lax.rem(begin + odd + 2 * i, units), 256) for i in range(4)]
+    pieces_left.append((lax.rem(begin + 8 * (1 - odd), units), 128))
 
     for i in range(n_event - 1):
         squash_copy(i).wait_recv()
     squash = jnp.concatenate([squash_all[e] for e in range(n_event)], axis=1)
     rough = 0.02 + 0.08 * squash
     rate = k_base / rough
+    slot_rate = pick([jnp.broadcast_to(rate, (16, reaches))], take_send)[0][0:1]
     shrinks = []
     for t in range(STEPS):
         area, p = areas[t], powers[t]
         flow = rate * area * p
-        if t > 0:
-            send(t, pick(flow, take_send), 1)
         inflow = lateral[t]
         for d in range(1, 9):
             inflow = inflow + pltpu.roll(flow * masks[d - 1], d, 1)
         shrink = 1.0 / (1.0 + beta * rate * p)
         shrinks.append(shrink)
+        kept = (area + beta * inflow) * shrink
+        gain = beta * shrink
+        if t < STEPS - 1:
+            slots = pick([kept, gain], take_send)
+        else:
+            loads["cotangent"].wait()
+            weight = cotangent[...] * rate * (5.0 / 3.0) * gain
+            slots = pick([kept, gain, weight], take_recv)
         if t > 0:
-            if t < n_event:
-                network(lax.rem(ev + t, n_event))
-            flow_in = scatter(receive(t, 1), take_recv)
-        inflow = inflow + flow_in
-        areas.append((area + beta * inflow) * shrink)
+            network(*pieces_left.pop(0))
+            got = receive(t, 1)
+        if t < STEPS - 1:
+            slot_area = slots[0] + slots[1] * cross(got, NT)
+            send(t + 1, slot_rate * slot_area * slot_power(slot_area), 1)
+        else:
+            slot_area = slots[0] + slots[1] * got
+            send(STEPS, slots[2] * slot_power(slot_area), -1)
+        areas.append(kept + gain * scatter(got, take_recv))
         powers.append(power(areas[t + 1]))
     emitted = areas[STEPS] * powers[STEPS]
     outflow[...] = rate * emitted
     write_flow = pltpu.make_async_copy(outflow, outflow_h, out_sem.at[0])
     write_flow.start()
-    loads["cotangent"].wait()
     g_area = cotangent[...] * rate * (5.0 / 3.0) * powers[STEPS]
     g_rate = cotangent[...] * emitted
     for t in reversed(range(STEPS)):
@@ -287,22 +322,28 @@
         inner = g_area * shrinks[t]
         g_inflow = inner * beta
         grad_lateral[t] = g_inflow
-        send(index, pick(g_inflow, take_recv), -1)
         g_flow = jnp.zeros((events, reaches), f32)
         for d in range(1, 9):
             g_flow = g_flow + masks[d - 1] * pltpu.roll(g_inflow, reaches - d, 1)
         drop = g_inflow * areas[t + 1] * powers[t]
-        g_rate = g_rate - drop
-        g_area = inner - (2.0 / 3.0) * rate * drop / areas[t]
-        if t == STEPS - 1:
-            for block in range(STEPS, n_event):
-                network(lax.rem(ev + block, n_event))
-        g_flow = g_flow + scatter(receive(index, -1), take_send)
-        g_rate = g_rate + g_flow * areas[t] * powers[t]
-        g_area = g_area + (5.0 / 3.0) * rate * powers[t] * g_flow
+        g_rate = g_rate - drop + g_flow * areas[t] * powers[t]
+        if t > 0:
+            lean = (5.0 / 3.0) * rate * powers[t]
+            onward = inner - (2.0 / 3.0) * rate * drop / areas[t] + lean * g_flow
+            gain = beta * shrinks[t - 1]
+            slots = pick([onward * gain, lean * gain], take_recv)
+            network(*pieces_left.pop(0))
+            got = receive(index, -1)
+            send(index + 1, slots[0] + slots[1] * cross(got, NN), -1)
+            back = scatter(got, take_send)
+            g_rate = g_rate + back * areas[t] * powers[t]
+            g_area = onward + lean * back
     write_lateral = pltpu.make_async_copy(grad_lateral, grad_lateral_h, out_sem.at[1])
     write_lateral.start()
-    rate_out[...] = jnp.sum(g_rate, axis=0, keepdims=True)
+    g_row = jnp.sum(g_rate, axis=0, keepdims=True)
+    network(*pieces_left.pop(0))
+    got = jnp.sum(receive(2 * STEPS - 1, -1) * slot_plain, axis=0, keepdims=True)
+    rate_out[...] = g_row + scatter(jnp.broadcast_to(got, (16, LINKS * GROUP)), take_send)[0:1]
 
     def rate_copy(i):
         return pltpu.make_async_remote_copy(
@@ -339,6 +380,66 @@
                 top = d * chunk + 8 * r
                 slab[d, r * tiles + c] = large[top : top + 8, 128 * c : 128 * c + 128]
 
+    def when_owner(index, work):
+        if owners == n:
+            work()
+        else:
+            pl.when(index < owners)(work)
+
+    line = n // 2
+    low = lax.rem(me, 2)
+    spot = me // 2
+    pair = me + 1 - 2 * low
+    half = lax.rem(ev + n_event // 2, n_event)
+    twin = ev + 1 - 2 * lax.rem(ev, 2)
+    twin_half = lax.rem(twin + n_event // 2, n_event)
+    span = slab.shape[1]
+    cut = (span + 1) // 2
+    halves = (pl.ds(0, cut), pl.ds(cut, span - cut))
+
+    def each(first, last, work):
+        if last - first <= 4:
+            for j in range(first, last):
+                work(j)
+        else:
+            pl.loop(first, last)(work)
+
+    def near(j):
+        if line != 4:
+            return lax.rem(spot + j, line)
+        if isinstance(j, int) and j == 0:
+            return spot
+        orders = ((1, 2, 3), (2, 0, 3), (1, 3, 0), (2, 1, 0))
+        code = sum(orders[s][j - 1] * 4 ** s for s in range(4))
+        power_of = (1 + 3 * lax.rem(spot, 2)) * (1 + 15 * (spot // 2))
+        return lax.rem(code // power_of, 4)
+
+    def device(z, parity):
+        return 2 * z + parity
+
+    def pair_sum(h, z, parity):
+        return pltpu.make_async_remote_copy(
+            src_ref=slab.at[device(z, parity), halves[h]], dst_ref=rs_pair.at[z, halves[h]],
+            send_sem=px_send.at[h, z], recv_sem=px_recv.at[h, z],
+            device_id={"basin": pair}, device_id_type=MESH,
+        )
+
+    def line_sum(h, z, sender):
+        return pltpu.make_async_remote_copy(
+            src_ref=rs_pair.at[z, halves[h]], dst_ref=rs_line.at[sender, halves[h]],
+            send_sem=pz_send.at[h, z], recv_sem=pz_recv.at[h, sender],
+            device_id={"basin": device(z, low)}, device_id_type=MESH,
+        )
+
+    def far(j):
+        return near(line - 1 - j)
+
+    def start_pair(h, j):
+        z = far(j)
+        when_owner(device(z, 1 - low), lambda: pair_sum(h, z, 1 - low).start())
+
+    each(0, line, functools.partial(start_pair, 0))
+
     g_pre = (lower[...] * g_logit32).astype(bf16)
     place = lax.broadcasted_iota(jnp.int32, (PLACES, reaches), 0)
     row_two = jnp.where(place == feat + 1, g_logit32, 0.0).astype(bf16)
@@ -346,12 +447,12 @@
     g_two = d_two[mine, :]
     second = h_two[mine, :]
 
-    def narrow(low):
-        high = low + 128
+    def narrow(first):
+        end = first + 128
         return (
-            lax.dot_general(attrs[...], g_pre[low:high], NT, preferred_element_type=f32)
-            + lax.dot_general(row_two, g_two[low:high], NT, preferred_element_type=f32)
-            + lax.dot_general(row_out, second[low:high], NT, preferred_element_type=f32)
+            lax.dot_general(attrs[...], g_pre[first:end], NT, preferred_element_type=f32)
+            + lax.dot_general(row_two, g_two[first:end], NT, preferred_element_type=f32)
+            + lax.dot_general(row_out, second[first:end], NT, preferred_element_type=f32)
         )
 
     left = narrow(0)
@@ -366,66 +467,7 @@
     for d in range(8, owners):
         slab[d, last] = jnp.zeros((8, 128), f32)
 
-    def when_owner(index, work):
-        if owners == n:
-            work()
-        else:
-            pl.when(index < owners)(work)
-
-    line = n // 2
-    low = lax.rem(me, 2)
-    spot = me // 2
-    pair = me + 1 - 2 * low
-    half = lax.rem(ev + n_event // 2, n_event)
-    twin = ev + 1 - 2 * lax.rem(ev, 2)
-    twin_half = lax.rem(twin + n_event // 2, n_event)
-    span = slab.shape[1]
-    cut = (span + 1) // 2
-    halves = (pl.ds(0, cut), pl.ds(cut, span - cut))
-
-    def each(first, last, work):
-        if last - first <= 4:
-            for j in range(first, last):
-                work(j)
-        else:
-            pl.loop(first, last)(work)
-
-    def near(j):
-        if line != 4:
-            return lax.rem(spot + j, line)
-        if isinstance(j, int) and j == 0:
-            return spot
-        orders = ((1, 2, 3), (2, 0, 3), (1, 3, 0), (2, 1, 0))
-        code = sum(orders[s][j - 1] * 4 ** s for s in range(4))
-        power_of = (1 + 3 * lax.rem(spot, 2)) * (1 + 15 * (spot // 2))
-        return lax.rem(code // power_of, 4)
-
-    def device(z, parity):
-        return 2 * z + parity
-
-    def pair_sum(h, z, parity):
-        return pltpu.make_async_remote_copy(
-            src_ref=slab.at[device(z, parity), halves[h]], dst_ref=rs_pair.at[z, halves[h]],
-            send_sem=px_send.at[h, z], recv_sem=px_recv.at[h, z],
-            device_id={"basin": pair}, device_id_type=MESH,
-        )
-
-    def line_sum(h, z, sender):
-        return pltpu.make_async_remote_copy(
-            src_ref=rs_pair.at[z, halves[h]], dst_ref=rs_line.at[sender, halves[h]],
-            send_sem=pz_send.at[h, z], recv_sem=pz_recv.at[h, sender],
-            device_id={"basin": device(z, low)}, device_id_type=MESH,
-        )
-
-    def far(j):
-        return near(line - 1 - j)
-
-    def start_pair(h, j):
-        z = far(j)
-        when_owner(device(z, 1 - low), lambda: pair_sum(h, z, 1 - low).start())
-
-    for h in range(2):
-        each(0, line, functools.partial(start_pair, h))
+    each(0, line, functools.partial(start_pair, 1))
 
     for i in range(n_event - 1):
         squash_copy(i).wait_send()
@@ -613,7 +655,7 @@
 def finish(
     feat, full_in, flow_in, lateral_in,
     large, flow_out, lateral_out, w_first, b_first, b_second, w_out,
-    full, flow, lateral, sems,
+    full, flow, lateral, small, vectors, sems, small_sems,
 ):
     last = full.shape[2] - 1
     middle = full.shape[0] // 2
@@ -647,11 +689,14 @@
             ]
         rows = jnp.concatenate(columns, axis=1)
         if k < 4:
-            w_first[8 * k : 8 * k + 8, :] = rows
+            small[8 * k : 8 * k + 8, :] = rows
         else:
-            b_first[...] = rows[0:1].reshape(rows.shape[1])
-            b_second[...] = rows[1:2].reshape(rows.shape[1])
-            w_out[...] = rows[2:3].reshape(rows.shape[1])
+            for i, held in enumerate(vectors):
+                held[...] = rows[i : i + 1].reshape(rows.shape[1])
+    pairs = [(small, w_first)] + list(zip(vectors, (b_first, b_second, w_out)))
+    for i, (held, target) in enumerate(pairs):
+        copies.append(pltpu.make_async_copy(held, target, small_sems.at[i]))
+        copies[-1].start()
     for copy in copies:
         copy.wait()
 
@@ -720,6 +765,7 @@
             pltpu.VMEM((n_event, 1, reaches // n_event), f32),
             pltpu.VMEM((LINKS * GROUP, reaches), bf16),
             pltpu.VMEM((LINKS * GROUP, reaches), bf16),
+            pltpu.VMEM((LINKS * GROUP, LINKS * GROUP), bf16),
             pltpu.VMEM((HALO + 1, LINKS, 8, 128), f32),
             pltpu.VMEM((HALO + 1, LINKS, 8, 128), f32),
             pltpu.VMEM((1, reaches), f32),
@@ -745,20 +791,24 @@
         area_start, lateral, cotangent,
     )
     vector = jax.ShapeDtypeStruct((hid,), f32)
+    w_first_f32 = jax.ShapeDtypeStruct((feat, hid), f32)
     large, outflow, grad_lateral, g_first, g_b_first, g_b_second, g_out = pl.pallas_call(
         functools.partial(finish, feat),
         out_shape=(
             jax.ShapeDtypeStruct((n_event, owners, span - 1, 8, 128), f32),
             jax.ShapeDtypeStruct((events, reaches), f32),
             jax.ShapeDtypeStruct((STEPS, events, reaches), f32),
-            jax.ShapeDtypeStruct((feat, hid), f32),
+            w_first_f32,
             vector,
             vector,
             vector,
         ),
         in_specs=[hbm] * 3,
-        out_specs=(hbm, hbm, hbm, vmem, vmem, vmem, vmem),
-        scratch_shapes=[held(full), held(outflow), held(grad_lateral), dma((2, 4))],
+        out_specs=(hbm,) * 7,
+        scratch_shapes=[
+            held(full), held(outflow), held(grad_lateral),
+            held(w_first_f32), [held(vector)] * 3, dma((2, 4)), dma((4,)),
+        ],
     )(full, outflow, grad_lateral)
     g_second = large.reshape(hid // 8, hid // 128, 8, 128).transpose(0, 2, 1, 3).reshape(hid, hid)
     return outflow, grad_lateral, g_first, g_b_first, g_second, g_b_second, g_out

time: 75 us -> 71.8 us (0.957)
  Pallas kernels: 73.3 us -> 70.1 us
    pallas_call x1, Pallas kernels: 69.6 us -> 67.1 us  [body(): pl.pallas_call(functools.partial(kernel, n, n_event, owners, chunk, scale...]
where the time goes in v4:
time: 71.8 us; the launch traced here: 70.8 us
  Pallas kernels  70.1 us (98%)
    pallas_call x1, Pallas kernels, body(): pl.pallas_call(functools.partial(kernel, n, n_event, owners, chunk, scale...  67.1 us
    pallas_call x1, Pallas kernels, body(): pl.pallas_call(functools.partial(finish, feat), out_shape=(jax.ShapeDtype...  3.08 us

profile of v4, /device:TPU:9, one launch (start us, length us, event | category | flops | bytes accessed | tf_op | source)
XLA Modules:
  0.0 70.8 jit_solution(11823748565431731078)
XLA Ops:
  0.6 67.1 %shard_map.207 = (f32[32,1536]{1,0:T(8,128)}, f32[3,32,1536]{2,1,0:T(8,128)}, f32[4,8,19,8,128]{4,3,2,1,0:T(8,128)}) custom-call(bf16[32,1536]{1,0:T(8,128)(2,1)} %bitcast.6, bf16[32,768]{1,0:T(8,128)(2,1)} %w_first_h.1, f32[768]{0:T(1024)} %b_first_h.1, bf16[768,768]{1,0:T(8,128)(2,1)} %w_second_h.1, f32[768]{0:T(1024)} %b_second_h.1, ...), custom_call_target="tpu_custom_call" | custom-call | tf_op jit(solution)/shard_map/pallas_call | solution.py:738
  67.7 3.1 %shard_map.208 = (f32[4,8,18,8,128]{4,3,2,1,0:T(8,128)}, f32[32,1536]{1,0:T(8,128)}, f32[3,32,1536]{2,1,0:T(8,128)}, f32[32,768]{1,0:T(8,128)}, f32[768]{0:T(1024)}, /*index=5*/f32[768]{0:T(1024)}, f32[768]{0:T(1024)}) custom-call(f32[4,8,19,8,128]{4,3,2,1,0:T(8,128)} %get-tuple-element.17.full_in, f32[32,1536]{1,0:T(8,128)} %get-tuple-element.18.flow_in, ...), custom_call_target="tpu_custom_call" | custom-call | tf_op jit(solution)/shard_map/pallas_call | solution.py:795

commit v5 on v4

--- a/solution.py
+++ b/solution.py
@@ -37,7 +37,7 @@
     area_start, lateral, cotangent, load_sem,
     w_firstT, w_secondT, cols,
     t_one, h_one, d_two, h_two, lower, squash_all, take_send, take_recv, overlap,
-    out_msg, in_msg, rate_out, rate_in, slab, rs_pair, rs_line,
+    out_msg, in_msg, share_out, share_in, share_send, share_recv, rate_out, rate_in, slab, rs_pair, rs_line,
     s_send, s_recv,
     x_send, x_recv, r_send, r_recv, px_send, px_recv, pz_send, pz_recv,
     az_send, az_recv, ax_send, ax_recv, ay_send, ay_recv,
@@ -57,9 +57,18 @@
 
     barrier = pltpu.get_barrier_semaphore()
 
-    @pl.loop(1, n)
-    def _(i):
-        pl.semaphore_signal(barrier, inc=1, device_id={"basin": lax.rem(me + i, n)}, device_id_type=MESH)
+    def greet(offset):
+        pl.semaphore_signal(
+            barrier, inc=1, device_id={"basin": lax.rem(me + offset, n)}, device_id_type=MESH
+        )
+
+    greet(1)
+    greet(n - 1)
+    if n <= 8:
+        for i in range(1, n // 2):
+            greet(2 * i)
+    else:
+        pl.loop(1, n // 2)(lambda i: greet(2 * i))
 
     for i in range(1, n_event):
         pl.semaphore_signal(
@@ -193,10 +202,10 @@
     areas = [area_start[...]]
     powers = [power(areas[0])]
     plain = areas[0] * powers[0]
-    outer, slot_plain = pick([k_base * plain, plain], take_send)
+    outer = pick([k_base * plain], take_send)[0]
     inputs = lax.dot_general(attrs[0:feat, :], take_send[...], NT, preferred_element_type=f32)
 
-    pl.semaphore_wait(barrier, n - 1 + n_event - 1)
+    pl.semaphore_wait(barrier, n // 2 + 1 + n_event - 1)
     send(HALO, inputs, 1)
     send(0, outer, 1)
 
@@ -283,6 +292,28 @@
     rough = 0.02 + 0.08 * squash
     rate = k_base / rough
     slot_rate = pick([jnp.broadcast_to(rate, (16, reaches))], take_send)[0][0:1]
+    first_got = got
+
+    def share(k, e):
+        return pltpu.make_async_remote_copy(
+            src_ref=share_out,
+            dst_ref=share_in.at[k, ev],
+            send_sem=share_send.at[k, e],
+            recv_sem=share_recv.at[k, ev],
+            device_id={"basin": lax.rem(me + n - offsets[k], n), "event": e},
+            device_id_type=MESH,
+        )
+
+    def shared_from(k, e):
+        return pltpu.make_async_remote_copy(
+            src_ref=share_out,
+            dst_ref=share_in.at[k, e],
+            send_sem=share_send.at[k, e],
+            recv_sem=share_recv.at[k, e],
+            device_id={"basin": lax.rem(me + n - offsets[k], n), "event": e},
+            device_id_type=MESH,
+        )
+
     shrinks = []
     for t in range(STEPS):
         area, p = areas[t], powers[t]
@@ -334,16 +365,20 @@
             slots = pick([onward * gain, lean * gain], take_recv)
             network(*pieces_left.pop(0))
             got = receive(index, -1)
-            send(index + 1, slots[0] + slots[1] * cross(got, NN), -1)
+            onto = slots[0] + slots[1] * cross(got, NN)
+            if t > 1:
+                send(index + 1, onto, -1)
+            else:
+                share_out[...] = jnp.sum(onto * first_got, axis=0, keepdims=True)
+                for k in range(LINKS):
+                    for e in range(n_event):
+                        share(k, e).start()
             back = scatter(got, take_send)
             g_rate = g_rate + back * areas[t] * powers[t]
             g_area = onward + lean * back
     write_lateral = pltpu.make_async_copy(grad_lateral, grad_lateral_h, out_sem.at[1])
     write_lateral.start()
-    g_row = jnp.sum(g_rate, axis=0, keepdims=True)
-    network(*pieces_left.pop(0))
-    got = jnp.sum(receive(2 * STEPS - 1, -1) * slot_plain, axis=0, keepdims=True)
-    rate_out[...] = g_row + scatter(jnp.broadcast_to(got, (16, LINKS * GROUP)), take_send)[0:1]
+    rate_out[...] = jnp.sum(g_rate, axis=0, keepdims=True)
 
     def rate_copy(i):
         return pltpu.make_async_remote_copy(
@@ -357,8 +392,19 @@
 
     for i in range(n_event - 1):
         rate_copy(i).start()
+    network(*pieces_left.pop(0))
     for i in range(n_event - 1):
         rate_copy(i).wait_recv()
+    slot_group = lax.broadcasted_iota(jnp.int32, (1, LINKS * GROUP), 1) // GROUP
+    shares = jnp.zeros((1, LINKS * GROUP), f32)
+    for k in range(LINKS):
+        for e in range(n_event):
+            shared_from(k, e).wait_recv()
+        total = share_in[k, 0]
+        for e in range(1, n_event):
+            total = total + share_in[k, e]
+        shares = jnp.where(slot_group == k, total, shares)
+    shared = scatter(jnp.broadcast_to(shares, (16, LINKS * GROUP)), take_send)[0:1] / rate
     terms = [rate_out[...]] + [rate_in[i] for i in range(n_event - 1)]
     g_sum = jnp.zeros((1, reaches), f32)
     for e in range(n_event):
@@ -366,6 +412,7 @@
         for i in range(n_event - 1):
             term = jnp.where(lax.rem(e + 1 + i, n_event) == ev, terms[i + 1], term)
         g_sum = g_sum + term
+    g_sum = g_sum + shared
     g_logit = (
         g_sum * (-rate / rough) * (scale * 0.08) * squash * (1.0 - squash)
     ).astype(bf16)
@@ -473,7 +520,11 @@
         squash_copy(i).wait_send()
     for index in range(HALO + 1):
         for k in range(LINKS):
-            message(index, k, 1).wait_send()
+            if index != 2 * STEPS - 1:
+                message(index, k, 1).wait_send()
+    for k in range(LINKS):
+        for e in range(n_event):
+            share(k, e).wait_send()
     for i in range(n_event - 1):
         rate_copy(i).wait_send()
     write_flow.wait()
@@ -632,8 +683,6 @@
 
         when_owner(2 * z, go)
 
-    each(0, line, drain)
-
     def write_full(z):
         where = pl.ds(2 * z, 2)
         return pltpu.make_async_copy(full.at[:, where], full_h.at[:, where], write_sem.at[z])
@@ -649,6 +698,7 @@
         when_owner(2 * z, go)
 
     each(0, line, arrive)
+    each(0, line, drain)
     each(0, line, lambda j: when_owner(2 * near(j), lambda: write_full(near(j)).wait()))
 
 
@@ -768,6 +818,10 @@
             pltpu.VMEM((LINKS * GROUP, LINKS * GROUP), bf16),
             pltpu.VMEM((HALO + 1, LINKS, 8, 128), f32),
             pltpu.VMEM((HALO + 1, LINKS, 8, 128), f32),
+            pltpu.VMEM((1, LINKS * GROUP), f32),
+            pltpu.VMEM((LINKS, n_event, 1, LINKS * GROUP), f32),
+            dma((LINKS, n_event)),
+            dma((LINKS, n_event)),
             pltpu.VMEM((1, reaches), f32),
             pltpu.VMEM((n_event - 1, 1, reaches), f32),
             pltpu.VMEM((owners, span, 8, 128), f32),

time: 71.8 us -> 68.5 us (0.954)
  Pallas kernels: 70.1 us -> 67 us
    pallas_call x1, Pallas kernels: 67.1 us -> 63.9 us  [body(): pl.pallas_call(functools.partial(kernel, n, n_event, owners, chunk, scale...]
where the time goes in v5:
time: 68.5 us; the launch traced here: 67.6 us
  Pallas kernels  67 us (98%)
    pallas_call x1, Pallas kernels, body(): pl.pallas_call(functools.partial(kernel, n, n_event, owners, chunk, scale...  63.9 us
    pallas_call x1, Pallas kernels, body(): pl.pallas_call(functools.partial(finish, feat), out_shape=(jax.ShapeDtype...  3.08 us

profile of v5, /device:TPU:9, one launch (start us, length us, event | category | flops | bytes accessed | tf_op | source)
XLA Modules:
  0.0 67.6 jit_solution(1246067207154605295)
XLA Ops:
  0.6 63.9 %shard_map.207 = (f32[32,1536]{1,0:T(8,128)}, f32[3,32,1536]{2,1,0:T(8,128)}, f32[4,8,19,8,128]{4,3,2,1,0:T(8,128)}) custom-call(bf16[32,1536]{1,0:T(8,128)(2,1)} %bitcast.6, bf16[32,768]{1,0:T(8,128)(2,1)} %w_first_h.1, f32[768]{0:T(1024)} %b_first_h.1, bf16[768,768]{1,0:T(8,128)(2,1)} %w_second_h.1, f32[768]{0:T(1024)} %b_second_h.1, ...), custom_call_target="tpu_custom_call" | custom-call | tf_op jit(solution)/shard_map/pallas_call | solution.py:788
  64.6 3.1 %shard_map.208 = (f32[4,8,18,8,128]{4,3,2,1,0:T(8,128)}, f32[32,1536]{1,0:T(8,128)}, f32[3,32,1536]{2,1,0:T(8,128)}, f32[32,768]{1,0:T(8,128)}, f32[768]{0:T(1024)}, /*index=5*/f32[768]{0:T(1024)}, f32[768]{0:T(1024)}) custom-call(f32[4,8,19,8,128]{4,3,2,1,0:T(8,128)} %get-tuple-element.17.full_in, f32[32,1536]{1,0:T(8,128)} %get-tuple-element.18.flow_in, ...), custom_call_target="tpu_custom_call" | custom-call | tf_op jit(solution)/shard_map/pallas_call | solution.py:849

commit v6 on v5

--- a/solution.py
+++ b/solution.py
@@ -87,11 +87,6 @@
         ("b_first", b_first_h, b_first),
         ("b_second", b_second_h, b_second),
         ("w_out", w_out_h, w_out),
-        ("recv_list", recv_list_h, recv_list),
-        ("seg_count", seg_count_h, seg_count),
-        ("down_local", down_local_h, down_local),
-        ("lateral", lateral_h, lateral),
-        ("cotangent", cotangent_h, cotangent),
     ):
         loads[name] = pltpu.make_async_copy(source, target, load_sem.at[len(loads)])
         loads[name].start()
@@ -208,6 +203,15 @@
     pl.semaphore_wait(barrier, n // 2 + 1 + n_event - 1)
     send(HALO, inputs, 1)
     send(0, outer, 1)
+    for name, source, target in (
+        ("recv_list", recv_list_h, recv_list),
+        ("seg_count", seg_count_h, seg_count),
+        ("down_local", down_local_h, down_local),
+        ("lateral", lateral_h, lateral),
+        ("cotangent", cotangent_h, cotangent),
+    ):
+        loads[name] = pltpu.make_async_copy(source, target, load_sem.at[len(loads)])
+        loads[name].start()
 
     for name in ("w_first", "b_first", "b_second", "w_out", "w_second"):
         loads[name].wait()
@@ -566,8 +570,8 @@
     def on_half(event, z):
         return move(event, device(z, 1 - low), 0, (fa_send, fa_recv), z, {"event": half})
 
-    def on_pair(z, parity):
-        return move(half, device(z, parity), 1, (fb_send, fb_recv), z, {"basin": pair})
+    def on_half_two(event, z):
+        return move(event, device(z, 1 - low), 1, (fb_send, fb_recv), z, {"event": half})
 
     def to_twin(side, event, z):
         ref = full.at[event, pl.ds(2 * z, 2)]
@@ -617,8 +621,8 @@
                 to_pair(0, z, 1 - low).wait_recv()
                 on_half(ev, z).start()
             else:
-                to_half(1, half, z).wait_recv()
-                on_pair(z, low).start()
+                to_pair(1, z, 1 - low).wait_recv()
+                on_half_two(ev, z).start()
 
         when_owner(2 * z, go)
 
@@ -626,11 +630,11 @@
         z = near(j)
 
         def go():
-            to_pair(1, z, 1 - low).wait_recv()
             to_twin(0, ev, z).start()
             to_half(0, half, z).wait_recv()
+            to_half(1, half, z).wait_recv()
             on_half(half, z).wait_recv()
-            on_pair(z, 1 - low).wait_recv()
+            on_half_two(half, z).wait_recv()
             to_twin(1, half, z).start()
 
         when_owner(2 * z, go)
@@ -661,9 +665,7 @@
             each(1, line, functools.partial(from_line, h))
         for h in range(2):
             each(0, line, functools.partial(hop, h))
-    each(0, line, corner)
-
-    def drain(z):
+    def settle(z):
         for h in range(2):
             when_owner(device(z, 1 - low), lambda: pair_sum(h, z, 1 - low).wait_send())
 
@@ -676,12 +678,21 @@
             for h in range(2):
                 to_pair(h, z, low).wait_send()
                 to_half(h, ev, z).wait_send()
+
+        when_owner(2 * z, go)
+
+    def drain(z):
+        def go():
             on_half(ev, z).wait_send()
-            on_pair(z, low).wait_send()
+            on_half_two(ev, z).wait_send()
             to_twin(0, ev, z).wait_send()
             to_twin(1, half, z).wait_send()
 
         when_owner(2 * z, go)
+
+    each(0, line - 1, corner)
+    each(0, line, settle)
+    corner(line - 1)
 
     def write_full(z):
         where = pl.ds(2 * z, 2)
@@ -708,10 +719,9 @@
     full, flow, lateral, small, vectors, sems, small_sems,
 ):
     last = full.shape[2] - 1
-    middle = full.shape[0] // 2
     steps = []
-    for side in range(2):
-        where = pl.ds(side * middle, middle)
+    for side in range(full.shape[0]):
+        where = pl.ds(side, 1)
         steps.append((full_in.at[where], full.at[where], full.at[where, :, pl.ds(0, last)], large.at[where]))
     steps.append((lateral_in, lateral, lateral, lateral_out))
     steps.append((flow_in, flow, flow, flow_out))
@@ -861,7 +871,7 @@
         out_specs=(hbm,) * 7,
         scratch_shapes=[
             held(full), held(outflow), held(grad_lateral),
-            held(w_first_f32), [held(vector)] * 3, dma((2, 4)), dma((4,)),
+            held(w_first_f32), [held(vector)] * 3, dma((2, n_event + 2)), dma((4,)),
         ],
     )(full, outflow, grad_lateral)
     g_second = large.reshape(hid // 8, hid // 128, 8, 128).transpose(0, 2, 1, 3).reshape(hid, hid)

time: 68.5 us -> 68.4 us (level)
  no operation moved by 1% of the time
where the time goes in v6:
time: 68.4 us; the launch traced here: 67.7 us
  Pallas kernels  67 us (98%)
    pallas_call x1, Pallas kernels, body(): pl.pallas_call(functools.partial(kernel, n, n_event, owners, chunk, scale...  64.2 us
    pallas_call x1, Pallas kernels, body(): pl.pallas_call(functools.partial(finish, feat), out_shape=(jax.ShapeDtype...  2.9 us

profile of v6, /device:TPU:9, one launch (start us, length us, event | category | flops | bytes accessed | tf_op | source)
XLA Modules:
  0.0 67.7 jit_solution(13658486902682917311)
XLA Ops:
  0.6 64.2 %shard_map.207 = (f32[32,1536]{1,0:T(8,128)}, f32[3,32,1536]{2,1,0:T(8,128)}, f32[4,8,19,8,128]{4,3,2,1,0:T(8,128)}) custom-call(bf16[32,1536]{1,0:T(8,128)(2,1)} %bitcast.6, bf16[32,768]{1,0:T(8,128)(2,1)} %w_first_h.1, f32[768]{0:T(1024)} %b_first_h.1, bf16[768,768]{1,0:T(8,128)(2,1)} %w_second_h.1, f32[768]{0:T(1024)} %b_second_h.1, ...), custom_call_target="tpu_custom_call" | custom-call | tf_op jit(solution)/shard_map/pallas_call | solution.py:798
  64.8 2.9 %shard_map.208 = (f32[4,8,18,8,128]{4,3,2,1,0:T(8,128)}, f32[32,1536]{1,0:T(8,128)}, f32[3,32,1536]{2,1,0:T(8,128)}, f32[32,768]{1,0:T(8,128)}, f32[768]{0:T(1024)}, /*index=5*/f32[768]{0:T(1024)}, f32[768]{0:T(1024)}) custom-call(f32[4,8,19,8,128]{4,3,2,1,0:T(8,128)} %get-tuple-element.17.full_in, f32[32,1536]{1,0:T(8,128)} %get-tuple-element.18.flow_in, ...), custom_call_target="tpu_custom_call" | custom-call | tf_op jit(solution)/shard_map/pallas_call | solution.py:859

commit v7 on v6

--- a/solution.py
+++ b/solution.py
@@ -279,6 +279,7 @@
             jnp.dot(weight[...], x, preferred_element_type=f32) + cols[:, column : column + 1]
         ).astype(bf16)
 
+    carried = [pltpu.roll(plain * masks[d - 1], d, 1) for d in range(1, 9)]
     around = receive(HALO, 1).astype(bf16)
     around = hidden_of(w_secondT, hidden_of(w_firstT, around, 0), 1)
     around = jnp.dot(w_out_rows, around, preferred_element_type=f32)[0:1]
@@ -324,7 +325,11 @@
         flow = rate * area * p
         inflow = lateral[t]
         for d in range(1, 9):
-            inflow = inflow + pltpu.roll(flow * masks[d - 1], d, 1)
+            if t == 0:
+                moved = pltpu.roll(jnp.broadcast_to(rate, (8, reaches)), d, 1)[0:1]
+                inflow = inflow + carried[d - 1] * moved
+            else:
+                inflow = inflow + pltpu.roll(flow * masks[d - 1], d, 1)
         shrink = 1.0 / (1.0 + beta * rate * p)
         shrinks.append(shrink)
         kept = (area + beta * inflow) * shrink
@@ -597,7 +602,7 @@
 
                 total = lax.fori_loop(1, line, add, total)
             full[ev, me, halves[h]] = total
-            each(1, line, lambda j: to_line(h, spot, near(j)).start())
+            each(1, line, lambda j: to_line(h, spot, near(line - j)).start())
             to_pair(h, spot, low).start()
             to_half(h, ev, spot).start()
 

time: 68.4 us -> 68.2 us (level)
  no operation moved by 1% of the time
where the time goes in v7:
time: 68.2 us; the launch traced here: 68 us
  Pallas kernels  67.4 us (99%)
    pallas_call x1, Pallas kernels, body(): pl.pallas_call(functools.partial(kernel, n, n_event, owners, chunk, scale...  64.5 us
    pallas_call x1, Pallas kernels, body(): pl.pallas_call(functools.partial(finish, feat), out_shape=(jax.ShapeDtype...  2.9 us

profile of v7, /device:TPU:9, one launch (start us, length us, event | category | flops | bytes accessed | tf_op | source)
XLA Modules:
  0.0 68.0 jit_solution(10330894950456188357)
XLA Ops:
  0.6 64.5 %shard_map.207 = (f32[32,1536]{1,0:T(8,128)}, f32[3,32,1536]{2,1,0:T(8,128)}, f32[4,8,19,8,128]{4,3,2,1,0:T(8,128)}) custom-call(bf16[32,1536]{1,0:T(8,128)(2,1)} %bitcast.6, bf16[32,768]{1,0:T(8,128)(2,1)} %w_first_h.1, f32[768]{0:T(1024)} %b_first_h.1, bf16[768,768]{1,0:T(8,128)(2,1)} %w_second_h.1, f32[768]{0:T(1024)} %b_second_h.1, ...), custom_call_target="tpu_custom_call" | custom-call | tf_op jit(solution)/shard_map/pallas_call | solution.py:803
  65.1 2.9 %shard_map.208 = (f32[4,8,18,8,128]{4,3,2,1,0:T(8,128)}, f32[32,1536]{1,0:T(8,128)}, f32[3,32,1536]{2,1,0:T(8,128)}, f32[32,768]{1,0:T(8,128)}, f32[768]{0:T(1024)}, /*index=5*/f32[768]{0:T(1024)}, f32[768]{0:T(1024)}) custom-call(f32[4,8,19,8,128]{4,3,2,1,0:T(8,128)} %get-tuple-element.17.full_in, f32[32,1536]{1,0:T(8,128)} %get-tuple-element.18.flow_in, ...), custom_call_target="tpu_custom_call" | custom-call | tf_op jit(solution)/shard_map/pallas_call | solution.py:864
